TPU v7x, 128 devices: a whole 4x4x4 slice. The times are simulated.
128 devices in a mesh: ctx: 32 (over x, z, y_lo), head: 4 (over y_hi, core).
Axes of the slice: x: 4, y: 4 (y_hi: 2, y_lo: 2; y = y_hi * 2 + y_lo), z: 4, core: 2. Of those that a mesh axis runs over, the one named last changes fastest.
Arguments:
- attn_query: bfloat16 [16384, 6144], P('ctx', 'head'), may hold values from -16 to 16
- attn_key: bfloat16 [16384, 6144], P('ctx', 'head'), may hold values from -16 to 16
- attn_value: bfloat16 [16384, 6144], P('ctx', 'head'), may hold values from -120 to 120
- delta_query: bfloat16 [16384, 6144], P('ctx', 'head'), may hold values from -6 to 6
- delta_key: bfloat16 [16384, 6144], P('ctx', 'head'), may hold values from -6 to 6
- delta_value: bfloat16 [16384, 6144], P('ctx', 'head'), may hold values from -120 to 120
- delta_gate: float32 [16384, 48], P('ctx', 'head'), may hold values from 0.5 to 1
- delta_beta: float32 [16384, 48], P('ctx', 'head'), may hold values from 0 to 0.6, as said below
- attn_gain: float32 [6144], P('head'), may hold values from 0.1 to 1.9
- delta_gain: float32 [6144], P('head'), may hold values from 0.1 to 1.9
Outputs:
- mixed: bfloat16 [16384, 6144], P('ctx', 'head')
Inputs may be any that keep to these rules, and one draw needn't show every extreme that they name: `delta_beta`: Positive.
All inputs are finite; a program needn't handle non-finite values.
Results may differ from a plain program's by a relative error of at most 0.004.
Values may be sent and summed in bfloat16 or wider, within the bound.
No kernel may reach another device: no remote copies, remote signals or barrier semaphores. Data moves between devices by JAX's collectives and lax.ppermute only.
A program may use at most 192 MiB of HBM per device.

v0:
```python
import functools
import math

import jax
import jax.numpy as jnp
from jax import lax
from jax.experimental import pallas as pl
from jax.experimental.pallas import tpu as pltpu
from jax.sharding import PartitionSpec as P

DH = 128
WIDTH = 6144
WINDOW = 1024
EPS = 1e-06
C = 128
HB = 2
PAY = 208
NEG = -1e30
f32 = jnp.float32
bf16 = jnp.bfloat16

NN = (((1,), (0,)), ((), ()))
NT = (((1,), (1,)), ((), ()))
TN = (((0,), (0,)), ((), ()))


def mm(a, b, dims=NN):
    return lax.dot_general(a, b, dims, preferred_element_type=f32)


def split(x):
    hi = x.astype(bf16)
    lo = (x - hi.astype(f32)).astype(bf16)
    return hi, lo


def cat(parts, axis):
    return jnp.concatenate(parts, axis=axis)


def dot3(a, b):
    (ah, al), (bh, bl) = a, b
    lhs = cat([ah, al], 1)
    rhs = cat([cat([bh, bl], 1), cat([bh, jnp.zeros_like(bl)], 1)], 0)
    r = mm(lhs, rhs)
    return r[:, :C] + r[:, C:]


def wide3(a, b):
    (ah, al), (bh, bl) = a, b
    return mm(cat([ah, al], 1), cat([bh, bh], 0)) + mm(ah, bl)


def delta_kernel(q_ref, k_ref, v_ref, g_ref, b_ref, o_ref, y_ref, pay_ref):
    rows = q_ref.shape[0]
    nc = rows // C
    units = HB * nc
    ri = lax.broadcasted_iota(jnp.int32, (C, C), 0)
    ci = lax.broadcasted_iota(jnp.int32, (C, C), 1)
    eye = ri == ci
    lower = ri >= ci
    xor = jnp.where(ri > ci, ri ^ ci, 0)
    triu = jnp.where(ri <= ci, 1.0, 0.0).astype(f32)
    identity = jnp.where(eye, 1.0, 0.0).astype(f32)

    def rows_of(ref):
        return cat([ref[hh][:, c * C : (c + 1) * C] for hh in range(HB) for c in range(nc)], 0)

    def tile(ref, hh, c):
        return ref[c * C : (c + 1) * C, hh * DH : (hh + 1) * DH]

    pairs = [(hh, c) for hh in range(HB) for c in range(nc)]
    logs = lax.dot_general(
        jnp.log(rows_of(g_ref)), triu, NN, precision=lax.Precision.HIGHEST, preferred_element_type=f32
    )
    beta = rows_of(b_ref)
    grams = []
    for hh, c in pairs:
        k = tile(k_ref, hh, c)
        grams.append(mm(cat([k, tile(q_ref, hh, c)], 0), k, NT))
    diag = cat([jnp.sum(jnp.where(eye, g[:C], 0.0), axis=0, keepdims=True) for g in grams], 0)
    key_scale = lax.rsqrt(diag * (1.0 / DH) + EPS) * (1.0 / math.sqrt(DH))
    growth = jnp.exp(logs)
    last = logs[:, C - 1 : C]
    decay = jnp.exp(last)
    tail = jnp.exp(last - logs) * key_scale
    bs = beta * key_scale
    logs_c, growth_c, tail_c, bs_c, beta_c, bgs_c = (
        jnp.transpose(x) for x in (logs, growth, tail, bs, beta, bs * growth)
    )

    negs, mixes, invs = [], [], []
    for u, (hh, c) in enumerate(pairs):
        col = slice(u, u + 1)
        ratio = jnp.exp(jnp.where(lower, logs_c[:, col] - logs[col, :], NEG)) * key_scale[col, :]
        neg = jnp.where(xor > 0, grams[u][:C] * ratio * (-bs_c[:, col]), 0.0)
        mixes.append(split(grams[u][C:] * ratio))
        negs.append(split(neg))
        invs.append(identity + jnp.where(xor == 1, neg, 0.0))
    for level in range(1, C.bit_length() - 1):
        mask = (xor >> level) == 1
        parts = [split(t) for t in invs]
        left = [dot3(parts[u], negs[u]) for u in range(units)]
        both = [dot3(split(left[u]), parts[u]) for u in range(units)]
        invs = [invs[u] + jnp.where(mask, both[u], 0.0) for u in range(units)]
    invs = [split(t) for t in invs]

    zero = jnp.zeros((C, DH), f32)
    states = [None] * HB
    for c in range(nc):
        for hh in range(HB):
            u = hh * nc + c
            col = slice(u, u + 1)
            k, q, v = tile(k_ref, hh, c), tile(q_ref, hh, c), tile(v_ref, hh, c)
            vb = cat([v.astype(f32) * beta_c[:, col], zero], 1)
            if c == 0:
                ks = cat([zero, k.astype(f32)], 1)
                qs = cat([zero, q.astype(f32)], 1)
            else:
                sh, sl = split(states[hh])
                kq = cat([k, q], 0)
                both = mm(cat([kq, kq], 1), cat([sh, sl], 0))
                ks, qs = both[:C], both[C:]
            err = wide3(invs[u], split(vb - bgs_c[:, col] * ks))
            out = growth_c[:, col] * qs + wide3(mixes[u], split(err))
            qf = q.astype(f32)
            q_scale = lax.rsqrt(jnp.mean(qf * qf, axis=1, keepdims=True) + EPS) * (1.0 / math.sqrt(DH))
            out = out * q_scale
            o_ref[c * C : (c + 1) * C, hh * DH : (hh + 1) * DH] = out[:, :DH]
            y_ref[c * C : (c + 1) * C, hh * DH : (hh + 1) * DH] = out[:, DH:]
            eh, el = split(err * tail_c[:, col])
            new = mm(cat([k, k], 0), cat([eh, el], 0), TN)
            if c == 0:
                start = cat([zero, identity], 1)
                states[hh] = new + decay[u : u + 1, :] * start
            else:
                states[hh] = new + decay[u : u + 1, :] * states[hh]

    row16 = lax.broadcasted_iota(jnp.int32, (16, DH), 0)
    for hh in range(HB):
        total = decay[hh * nc : hh * nc + 1, :]
        for c in range(1, nc):
            total = total * decay[hh * nc + c : hh * nc + c + 1, :]
        linear = (states[hh][:, DH:] - total * identity).astype(bf16)
        offset = jnp.transpose(states[hh][:, :DH]).astype(bf16)
        wide = jnp.broadcast_to(total, (16, DH))
        th = wide.astype(bf16).astype(f32)
        decays = jnp.where(row16 == 0, th, jnp.where(row16 == 1, wide - th, 0.0)).astype(bf16)
        for half in range(2):
            pay_ref[2 * hh + half, 0:128, :] = linear
            pay_ref[2 * hh + half, 128:192, :] = offset[half * 64 : (half + 1) * 64]
            pay_ref[2 * hh + half, 192:208, :] = decays


def chain_kernel(in_ref, out_ref):
    n = in_ref.shape[0]
    state = jnp.zeros((64, DH), f32)
    for j in range(n):
        out_ref[j] = state
        if j == n - 1:
            break
        sh, sl = split(state)
        r = mm(cat([sh, sl], 0), in_ref[j, 0:128, :], NT)
        dec = in_ref[j, 192:208, :].astype(f32)
        total = dec[0:1] + dec[1:2]
        state = r[:64] + r[64:] + total * state + in_ref[j, 128:192, :].astype(f32)


def attn_kernel(idx_ref, q_ref, k0_ref, v0_ref, k1a_ref, v1a_ref, k1b_ref, v1b_ref, k2_ref, v2_ref, o_ref, s_ref, k1_ref, v1_ref):
    QB = 128
    rows = q_ref.shape[0]
    nb = rows // QB
    ctx = idx_ref[0]
    odd = lax.rem(ctx, 2) == 1
    scale = math.log2(math.e) / math.sqrt(DH)

    @pl.when(odd)
    def _():
        k1_ref[...] = k1a_ref[...]
        v1_ref[...] = v1a_ref[...]

    @pl.when(jnp.logical_not(odd))
    def _():
        k1_ref[...] = k1b_ref[...]
        v1_ref[...] = v1b_ref[...]

    bias1 = jnp.where(ctx >= 1, 0.0, 1e30).astype(f32)
    bias2 = jnp.where(ctx >= 2, 0.0, 1e30).astype(f32)
    ri = lax.broadcasted_iota(jnp.int32, (QB, QB), 0)
    ci = lax.broadcasted_iota(jnp.int32, (QB, QB), 1)
    far = ci > ri

    @pl.when(pl.program_id(0) == 0)
    def _():
        s_ref[...] = jnp.zeros_like(s_ref)

    for b in range(nb):
        q = q_ref[b * QB : (b + 1) * QB, :]
        s2 = mm(q, k2_ref[b * QB :, :], NT)
        s1 = mm(q, k1_ref[...], NT)
        s0 = mm(q, k0_ref[: (b + 1) * QB, :], NT)
        st = jnp.where(far, s2[:, :QB] - bias2, s0[:, b * QB :])
        top = jnp.max(st, axis=1, keepdims=True)
        top = jnp.maximum(top, jnp.max(s1, axis=1, keepdims=True) - bias1)
        if b < nb - 1:
            s2 = s2[:, QB:]
            top = jnp.maximum(top, jnp.max(s2, axis=1, keepdims=True) - bias2)
        if b > 0:
            s0 = s0[:, : b * QB]
            top = jnp.maximum(top, jnp.max(s0, axis=1, keepdims=True))
        pt = jnp.exp2((st - top) * scale)
        p1 = jnp.exp2((s1 - (top + bias1)) * scale)
        total = jnp.sum(pt, axis=1, keepdims=True) + jnp.sum(p1, axis=1, keepdims=True)
        if b < nb - 1:
            p2 = jnp.exp2((s2 - (top + bias2)) * scale)
            total = total + jnp.sum(p2, axis=1, keepdims=True)
        if b > 0:
            p0 = jnp.exp2((s0 - top) * scale)
            total = total + jnp.sum(p0, axis=1, keepdims=True)
        inv = 1.0 / total
        pt = pt * inv
        w2 = jnp.where(far, pt, 0.0).astype(bf16)
        w0 = jnp.where(far, 0.0, pt).astype(bf16)
        if b < nb - 1:
            w2 = cat([w2, (p2 * inv).astype(bf16)], 1)
        if b > 0:
            w0 = cat([(p0 * inv).astype(bf16), w0], 1)
        w1 = (p1 * inv).astype(bf16)
        out = mm(w1, v1_ref[...]) + mm(w2, v2_ref[b * QB :, :]) + mm(w0, v0_ref[: (b + 1) * QB, :])
        o_ref[b * QB : (b + 1) * QB, :] = out
        s_ref[b * QB : (b + 1) * QB, :] += out * out


def apply_kernel(o_ref, y_ref, t_ref, d_ref, s_ref):
    yh, yl = split(y_ref[...])
    s = cat([t_ref[0], t_ref[1]], 0)
    sh, sl = split(s)
    out = o_ref[...] + mm(cat([yh, yl], 1), cat([sh, sh], 1), NT) + mm(yh, sl, NT)
    d_ref[...] = out

    @pl.when(pl.program_id(0) == 0)
    def _():
        s_ref[...] = jnp.zeros_like(s_ref)

    s_ref[...] += out * out


def join_kernel(sq_ref, a_ref, d_ref, ag_ref, dg_ref, o_ref):
    sq = sq_ref[...]
    scale = lax.rsqrt(sq * (1.0 / WIDTH) + EPS)
    o_ref[...] = (
        0.5 * (ag_ref[...] * a_ref[...] * scale[:, 0:1] + dg_ref[...] * d_ref[...] * scale[:, 1:2])
    ).astype(bf16)


def params(mb):
    return pltpu.CompilerParams(vmem_limit_bytes=mb * 2**20)


def on_device(aq, ak, av, dq, dk, dv, gate, beta, ag, dg):
    rows, width = aq.shape
    heads = gate.shape[1]
    nctx = lax.axis_size("ctx")
    index = lax.axis_index("ctx").astype(jnp.int32).reshape(1)

    hop = [(i, i + 2) for i in range(nctx - 2)]
    ahead = [(i, i + 1) for i in range(0, nctx, 2)]
    back = [(i, i - 1) for i in range(1, nctx, 2)]

    def send(x, pairs):
        return lax.ppermute(x, "ctx", pairs)

    k2, v2 = send(ak, hop), send(av, hop)
    k1a, v1a = send(ak, ahead), send(av, ahead)
    k1b, v1b = send(k2, back), send(v2, back)

    gt = gate.T.reshape(heads, 1, rows)
    bt = beta.T.reshape(heads, 1, rows)
    wide = pl.BlockSpec((rows, HB * DH), lambda h: (0, h))
    small = pl.BlockSpec((HB, 1, rows), lambda h: (h, 0, 0))
    local, effect, pay = pl.pallas_call(
        delta_kernel,
        grid=(heads // HB,),
        in_specs=[wide, wide, wide, small, small],
        out_specs=[wide, wide, pl.BlockSpec((2 * HB, PAY, DH), lambda h: (h, 0, 0))],
        out_shape=[
            jax.ShapeDtypeStruct((rows, width), f32),
            jax.ShapeDtypeStruct((rows, width), f32),
            jax.ShapeDtypeStruct((nctx, PAY, DH), bf16),
        ],
        compiler_params=params(48),
        cost_estimate=pl.CostEstimate(flops=30 * 10**9, bytes_accessed=12 * 2**20, transcendentals=10**6),
        name="delta_local",
    )(dq, dk, dv, gt, bt)

    got = lax.all_to_all(pay, "ctx", 0, 0, tiled=True)
    chain = pl.pallas_call(
        chain_kernel,
        out_shape=jax.ShapeDtypeStruct((nctx, 64, DH), f32),
        compiler_params=params(32),
        cost_estimate=pl.CostEstimate(flops=10**10, bytes_accessed=3 * 2**20, transcendentals=0),
        name="delta_chain",
    )(got)
    states = lax.all_to_all(chain, "ctx", 0, 0, tiled=True)

    one = pl.BlockSpec((rows, DH), lambda h: (0, h))
    fixed = pl.BlockSpec((rows, DH), lambda h: (0, 0))
    attn, attn_sq = pl.pallas_call(
        attn_kernel,
        grid=(heads,),
        in_specs=[pl.BlockSpec(memory_space=pltpu.SMEM)] + [one] * 9,
        out_specs=[one, fixed],
        out_shape=[
            jax.ShapeDtypeStruct((rows, width), f32),
            jax.ShapeDtypeStruct((rows, DH), f32),
        ],
        scratch_shapes=[pltpu.VMEM((rows, DH), bf16), pltpu.VMEM((rows, DH), bf16)],
        compiler_params=params(48),
        cost_estimate=pl.CostEstimate(flops=10**10, bytes_accessed=20 * 2**20, transcendentals=7 * 10**6),
        name="window_attention",
    )(index, aq, ak, av, k1a, v1a, k1b, v1b, k2, v2)

    delta, delta_sq = pl.pallas_call(
        apply_kernel,
        grid=(heads,),
        in_specs=[one, one, pl.BlockSpec((2, 64, DH), lambda h: (h, 0, 0))],
        out_specs=[one, fixed],
        out_shape=[
            jax.ShapeDtypeStruct((rows, width), f32),
            jax.ShapeDtypeStruct((rows, DH), f32),
        ],
        compiler_params=params(32),
        name="delta_apply",
    )(local, effect, states)

    squares = jnp.stack([jnp.sum(attn_sq, axis=1), jnp.sum(delta_sq, axis=1)], axis=1)
    squares = lax.psum(squares, "head")

    block = 256
    cols = pl.BlockSpec((block, width), lambda i: (i, 0))
    gains = pl.BlockSpec((1, width), lambda i: (0, 0))
    return pl.pallas_call(
        join_kernel,
        grid=(rows // block,),
        in_specs=[pl.BlockSpec((block, 2), lambda i: (i, 0)), cols, cols, gains, gains],
        out_specs=cols,
        out_shape=jax.ShapeDtypeStruct((rows, width), bf16),
        compiler_params=params(32),
        name="join",
    )(squares, attn, delta, ag.reshape(1, width), dg.reshape(1, width))


def solution(mesh):
    shard = P("ctx", "head")
    return jax.shard_map(
        on_device,
        mesh=mesh,
        in_specs=(shard,) * 8 + (P("head"), P("head")),
        out_specs=shard,
        check_vma=False,
    )
```

profile of v0, /device:TPU:84, one launch (start us, length us, event | category | flops | bytes accessed | tf_op | source)
XLA Modules:
  0.0 255.6 jit_solution(16596548327232830947)
XLA Ops:
  0.0 0.8 reshape.16.g_ref
  0.8 0.8 reshape.17.b_ref
  1.6 0.0 copy-start.5
  1.6 1.4 copy-done.5
  3.0 0.0 copy-start.6
  3.0 1.4 copy-done.6
  4.4 0.0 copy-start.7
  4.4 1.4 copy-done.7
  5.8 36.5 %delta_local.1 = (f32[512,1536]{1,0:T(8,128)}, f32[512,1536]{1,0:T(8,128)}, bf16[32,208,128]{2,1,0:T(8,128)(2,1)}) custom-call(bf16[512,1536]{1,0:T(8,128)(2,1)S(1)} %copy-done.5, bf16[512,1536]{1,0:T(8,128)(2,1)S(1)} %copy-done.6, bf16[512,1536]{1,0:T(8,128)(2,1)S(1)} %copy-done.7, f32[12,1,512]{2,1,0:T(1,128)S(1)} %reshape.16.g_ref, ...), custom_call_target="tpu_custom_call" | custom-call | flops 30000001024 | bytes 12582912 | tf_op jit(solution)/shard_map/delta_local/pallas_call | solution.py:281
  42.3 0.0 copy-start.9
  42.3 8.4 %all-to-all-start = ((bf16[32,208,128]{2,1,0:T(8,128)(2,1)}), bf16[32,208,128]{2,1,0:T(8,128)(2,1)S(1)}, u32[]{:S(2)}, u32[]{:S(2)}) async-start(bf16[32,208,128]{2,1,0:T(8,128)(2,1)} %get-tuple-element.15), calls=%async_computation | async-start | bytes 3407872 | tf_op jit(solution)/shard_map/all_to_all | solution.py:296
  50.7 0.0 copy-done.9
  50.7 3.1 %collective-permute-start.2 = (bf16[512,1536]{1,0:T(8,128)(2,1)S(1)}, bf16[512,1536]{1,0:T(8,128)(2,1)}, u32[]{:S(2)}, u32[]{:S(2)}) collective-permute-start(bf16[512,1536]{1,0:T(8,128)(2,1)S(1)} %copy-done.9), channel_id=1, source_target_pairs={{0,8},{4,12},{8,16},{12,20},{16,24},{20,28},{24,32},{28,36},{32,40... | collective-permute-start | bytes 4718600 | tf_op jit(solution)/shard_map/ppermute | solution.py:271
  53.8 3.1 %collective-permute-start.4 = (bf16[512,1536]{1,0:T(8,128)(2,1)}, bf16[512,1536]{1,0:T(8,128)(2,1)}, u32[]{:S(2)}, u32[]{:S(2)}) collective-permute-start(bf16[512,1536]{1,0:T(8,128)(2,1)} %v0_ref.1), channel_id=1, source_target_pairs={{0,8},{4,12},{8,16},{12,20},{16,24},{20,28},{24,32},{28,36},{32,40... | collective-permute-start | bytes 4718600 | tf_op jit(solution)/shard_map/ppermute | solution.py:271
  56.9 4.6 %collective-permute-start = (bf16[512,1536]{1,0:T(8,128)(2,1)S(1)}, bf16[512,1536]{1,0:T(8,128)(2,1)}, u32[]{:S(2)}, u32[]{:S(2)}) collective-permute-start(bf16[512,1536]{1,0:T(8,128)(2,1)S(1)} %copy-done.9), channel_id=1, source_target_pairs={{0,4},{8,12},{16,20},{24,28},{32,36},{40,44},{48,52},{56,60},{64,6... | collective-permute-start | bytes 4718600 | tf_op jit(solution)/shard_map/ppermute | solution.py:271
  61.5 2.4 collective-permute-start.1
  64.0 40.1 %collective-permute-done.2.k2_ref = bf16[512,1536]{1,0:T(8,128)(2,1)} collective-permute-done((bf16[512,1536]{1,0:T(8,128)(2,1)S(1)}, bf16[512,1536]{1,0:T(8,128)(2,1)}, u32[]{:S(2)}, u32[]{:S(2)}) %collective-permute-start.2) | collective-permute-done | bytes 1572896 | tf_op jit(solution)/shard_map/ppermute | solution.py:271
  104.0 1.3 collective-permute-start.3
  105.3 31.9 %collective-permute-done.4.v2_ref = bf16[512,1536]{1,0:T(8,128)(2,1)} collective-permute-done((bf16[512,1536]{1,0:T(8,128)(2,1)}, bf16[512,1536]{1,0:T(8,128)(2,1)}, u32[]{:S(2)}, u32[]{:S(2)}) %collective-permute-start.4) | collective-permute-done | bytes 1572896 | tf_op jit(solution)/shard_map/ppermute | solution.py:271
  137.2 1.3 collective-permute-start.5
  138.5 0.0 all-to-all-done.in_ref
  138.5 5.0 %delta_chain.1 = f32[32,64,128]{2,1,0:T(8,128)} custom-call(bf16[32,208,128]{2,1,0:T(8,128)(2,1)S(1)} %all-to-all-done.in_ref), custom_call_target="tpu_custom_call" | custom-call | flops 10000000000 | bytes 3145728 | tf_op jit(solution)/shard_map/delta_chain/pallas_call | solution.py:297
  143.5 0.0 copy-start.12
  143.5 0.0 copy-start.13
  143.5 11.5 %all-to-all-start.1 = ((f32[32,64,128]{2,1,0:T(8,128)}), f32[32,64,128]{2,1,0:T(8,128)S(1)}, u32[]{:S(2)}, u32[]{:S(2)}) async-start(f32[32,64,128]{2,1,0:T(8,128)} %delta_chain.1), calls=%async_computation.1 | async-start | bytes 2097152 | tf_op jit(solution)/shard_map/all_to_all | solution.py:304
  155.0 0.0 copy-done.12
  155.0 0.0 copy-done.13
  155.1 33.9 %all-to-all-done.1.t_ref = f32[32,64,128]{2,1,0:T(8,128)S(1)} async-done(((f32[32,64,128]{2,1,0:T(8,128)}), f32[32,64,128]{2,1,0:T(8,128)S(1)}, u32[]{:S(2)}, u32[]{:S(2)}) %all-to-all-start.1) | async-done | bytes 1048608 | tf_op jit(solution)/shard_map/all_to_all | solution.py:304
  189.0 0.0 copy-start
  189.0 1.9 copy-done
  190.9 0.0 copy-start.1
  190.9 1.9 copy-done.1
  192.8 4.9 %delta_apply.1 = (f32[512,1536]{1,0:T(8,128)S(1)}, f32[512,128]{1,0:T(8,128)S(1)}) custom-call(f32[512,1536]{1,0:T(8,128)S(1)} %copy-done, f32[512,1536]{1,0:T(8,128)S(1)} %copy-done.1, f32[32,64,128]{2,1,0:T(8,128)S(1)} %all-to-all-done.1.t_ref), custom_call_target="tpu_custom_call" | custom-call | tf_op jit(solution)/shard_map/delta_apply/pallas_call | solution.py:323
  197.7 0.0 copy-start.2
  197.7 1.7 copy-done.2
  199.3 0.1 reduce_sum.19
  199.5 0.0 collective-permute-done.k1a_ref
  199.5 0.0 collective-permute-done.1.v1a_ref
  199.5 0.0 collective-permute-done.3.k1b_ref
  199.5 0.0 collective-permute-done.5.v1b_ref
  199.5 0.0 copy-start.8
  199.5 1.4 copy-done.8
  200.9 0.0 copy-start.10
  200.9 1.4 copy-done.10
  202.3 0.0 copy-start.11
  202.3 1.4 copy-done.11
  203.8 0.0 copy-start.3
  203.8 29.8 %window_attention.1 = (f32[512,1536]{1,0:T(8,128)}, f32[512,128]{1,0:T(8,128)S(1)}) custom-call(s32[1]{0:T(128)} %bitcast.idx_ref, bf16[512,1536]{1,0:T(8,128)(2,1)S(1)} %copy-done.8, bf16[512,1536]{1,0:T(8,128)(2,1)S(1)} %copy-done.10, bf16[512,1536]{1,0:T(8,128)(2,1)S(1)} %copy-done.11, bf16[512,1536]{1,0:T(8,128)(2,1)} %collective-permute-done.k1a_ref, ...), custom_call_target="tpu_custom_call" | custom-call | flops 10000000000 | bytes 20971520 | tf_op jit(solution)/shard_map/window_attention/pallas_call | solution.py:308
  233.5 0.1 reduce_sum.18
  233.7 0.9 copy.13
  234.5 17.3 %psum.7.sq_ref = f32[512,2]{1,0:T(8,128)S(1)} all-reduce(f32[512,2]{1,0:T(8,128)} %copy.13), channel_id=1, replica_groups=mesh['ctx'=32,'head'=4] {'head'}, use_global_device_ids=true, to_apply=%region_2.0 | all-reduce | flops 1024 | bytes 8192 | tf_op jit(solution)/shard_map/psum | solution.py:337
  251.9 0.0 copy-done.3
  251.9 0.0 copy-start.4
  251.9 1.9 copy-done.4
  253.8 1.8 join.1
  (3 shorter events, 0.0 us)
Async XLA Ops:
  1.6 1.4 copy-start.5
  3.0 1.4 copy-start.6
  4.4 1.4 copy-start.7
  42.3 8.4 %copy-start.9 = (bf16[512,1536]{1,0:T(8,128)(2,1)S(1)}, bf16[512,1536]{1,0:T(8,128)(2,1)}, u32[]{:S(2)}) copy-start(bf16[512,1536]{1,0:T(8,128)(2,1)} %k0_ref.1) | copy-start | bytes 4718596
  42.3 96.2 %all-to-all-start = ((bf16[32,208,128]{2,1,0:T(8,128)(2,1)}), bf16[32,208,128]{2,1,0:T(8,128)(2,1)S(1)}, u32[]{:S(2)}, u32[]{:S(2)}) async-start(bf16[32,208,128]{2,1,0:T(8,128)(2,1)} %get-tuple-element.15), calls=%async_computation | async-start | bytes 3407872 | tf_op jit(solution)/shard_map/all_to_all | solution.py:296
  50.7 53.3 %collective-permute-start.2 = (bf16[512,1536]{1,0:T(8,128)(2,1)S(1)}, bf16[512,1536]{1,0:T(8,128)(2,1)}, u32[]{:S(2)}, u32[]{:S(2)}) collective-permute-start(bf16[512,1536]{1,0:T(8,128)(2,1)S(1)} %copy-done.9), channel_id=1, source_target_pairs={{0,8},{4,12},{8,16},{12,20},{16,24},{20,28},{24,32},{28,36},{32,40... | collective-permute-start | bytes 4718600 | tf_op jit(solution)/shard_map/ppermute | solution.py:271
  53.8 83.4 %collective-permute-start.4 = (bf16[512,1536]{1,0:T(8,128)(2,1)}, bf16[512,1536]{1,0:T(8,128)(2,1)}, u32[]{:S(2)}, u32[]{:S(2)}) collective-permute-start(bf16[512,1536]{1,0:T(8,128)(2,1)} %v0_ref.1), channel_id=1, source_target_pairs={{0,8},{4,12},{8,16},{12,20},{16,24},{20,28},{24,32},{28,36},{32,40... | collective-permute-start | bytes 4718600 | tf_op jit(solution)/shard_map/ppermute | solution.py:271
  56.9 142.6 %collective-permute-start = (bf16[512,1536]{1,0:T(8,128)(2,1)S(1)}, bf16[512,1536]{1,0:T(8,128)(2,1)}, u32[]{:S(2)}, u32[]{:S(2)}) collective-permute-start(bf16[512,1536]{1,0:T(8,128)(2,1)S(1)} %copy-done.9), channel_id=1, source_target_pairs={{0,4},{8,12},{16,20},{24,28},{32,36},{40,44},{48,52},{56,60},{64,6... | collective-permute-start | bytes 4718600 | tf_op jit(solution)/shard_map/ppermute | solution.py:271
  61.5 138.0 %collective-permute-start.1 = (bf16[512,1536]{1,0:T(8,128)(2,1)}, bf16[512,1536]{1,0:T(8,128)(2,1)}, u32[]{:S(2)}, u32[]{:S(2)}) collective-permute-start(bf16[512,1536]{1,0:T(8,128)(2,1)} %v0_ref.1), channel_id=1, source_target_pairs={{0,4},{8,12},{16,20},{24,28},{32,36},{40,44},{48,52},{56,60},{64,6... | collective-permute-start | bytes 4718600 | tf_op jit(solution)/shard_map/ppermute | solution.py:271
  104.0 95.5 %collective-permute-start.3 = (bf16[512,1536]{1,0:T(8,128)(2,1)}, bf16[512,1536]{1,0:T(8,128)(2,1)}, u32[]{:S(2)}, u32[]{:S(2)}) collective-permute-start(bf16[512,1536]{1,0:T(8,128)(2,1)} %collective-permute-done.2.k2_ref), channel_id=1, source_target_pairs={{4,0},{12,8},{20,16},{28,24},{36,32},{44,40},{52,48},{60,56},{68,6... | collective-permute-start | bytes 4718600 | tf_op jit(solution)/shard_map/ppermute | solution.py:271
  137.2 62.3 %collective-permute-start.5 = (bf16[512,1536]{1,0:T(8,128)(2,1)}, bf16[512,1536]{1,0:T(8,128)(2,1)}, u32[]{:S(2)}, u32[]{:S(2)}) collective-permute-start(bf16[512,1536]{1,0:T(8,128)(2,1)} %collective-permute-done.4.v2_ref), channel_id=1, source_target_pairs={{4,0},{12,8},{20,16},{28,24},{36,32},{44,40},{52,48},{60,56},{68,6... | collective-permute-start | bytes 4718600 | tf_op jit(solution)/shard_map/ppermute | solution.py:271
  143.5 11.5 %copy-start.12 = (f32[1536]{0:T(1024)S(1)}, f32[1536]{0:T(1024)}, u32[]{:S(2)}) copy-start(f32[1536]{0:T(1024)} %param.18) | copy-start | bytes 18436
  143.5 11.5 %copy-start.13 = (f32[1536]{0:T(1024)S(1)}, f32[1536]{0:T(1024)}, u32[]{:S(2)}) copy-start(f32[1536]{0:T(1024)} %param.19) | copy-start | bytes 18436
  143.5 45.4 %all-to-all-start.1 = ((f32[32,64,128]{2,1,0:T(8,128)}), f32[32,64,128]{2,1,0:T(8,128)S(1)}, u32[]{:S(2)}, u32[]{:S(2)}) async-start(f32[32,64,128]{2,1,0:T(8,128)} %delta_chain.1), calls=%async_computation.1 | async-start | bytes 2097152 | tf_op jit(solution)/shard_map/all_to_all | solution.py:304
  189.0 1.9 copy-start
  190.9 1.9 copy-start.1
  197.7 1.7 copy-start.2
  199.5 1.4 copy-start.8
  200.9 1.4 copy-start.10
  202.3 1.4 copy-start.11
  203.8 48.1 %copy-start.3 = (f32[512,1536]{1,0:T(8,128)S(1)}, f32[512,1536]{1,0:T(8,128)}, u32[]{:S(2)}) copy-start(f32[512,1536]{1,0:T(8,128)} %copy-done.2) | copy-start | bytes 9437188
  251.9 1.9 copy-start.4
where the time goes:
time: 258 us; the launch traced here: 256 us
  waiting for transfers between devices  106 us (41%)
  Pallas kernels  77.9 us (30%)
  starting transfers between devices  35.7 us (14%)
  local copies, waits for them, and re-layouts  18.2 us (7%)
  blocking collectives  17.3 us (7%)
    ppermute x6, waiting for transfers between devices, send(): return lax.ppermute(x, 'ctx', pairs)  72 us
    pallas_call x1, Pallas kernels, on_device(): pl.pallas_call(delta_kernel, grid=(heads // HB,), in_specs=[wide, wide, w...  36.5 us
    all_to_all x1, waiting for transfers between devices, on_device(): states = lax.all_to_all(chain, 'ctx', 0, 0, tiled=True)  33.9 us
    pallas_call x1, Pallas kernels, on_device(): pl.pallas_call(attn_kernel, grid=(heads,), in_specs=[pl.BlockSpec(memory_...  29.8 us
    psum x1, blocking collectives, on_device(): squares = lax.psum(squares, 'head')  17.3 us
    ppermute x6, starting transfers between devices, send(): return lax.ppermute(x, 'ctx', pairs)  15.8 us
    unnamed x28, local copies, waits for them, and re-layouts  15.8 us
    all_to_all x1, starting transfers between devices, on_device(): states = lax.all_to_all(chain, 'ctx', 0, 0, tiled=True)  11.5 us
  transfers between devices with their start and end apart: 8, of which 3 were waited for; matrix products, arithmetic and copies ran while one was open for 0% of the time, Pallas kernels for 4%

commit v1 on v0

v1 whole, which is shorter than its diff:
```python
import functools
import math

import jax
import jax.numpy as jnp
from jax import lax
from jax.experimental import pallas as pl
from jax.experimental.pallas import tpu as pltpu
from jax.sharding import PartitionSpec as P

DH = 128
WIDTH = 6144
WINDOW = 1024
EPS = 1e-06
C = 128
PARTS = (6, 4, 2)
AH = 2
QB = 256
COSTS = (2, 8, 5, 10, 5)
PAY = 208
NEG = -1e30
f32 = jnp.float32
bf16 = jnp.bfloat16

NN = (((1,), (0,)), ((), ()))
NT = (((1,), (1,)), ((), ()))
TN = (((0,), (0,)), ((), ()))


def mm(a, b, dims=NN):
    return lax.dot_general(a, b, dims, preferred_element_type=f32)


def split(x):
    hi = x.astype(bf16)
    lo = (x - hi.astype(f32)).astype(bf16)
    return hi, lo


def cat(parts, axis):
    return jnp.concatenate(parts, axis=axis)


def dot3(a, b):
    (ah, al), (bh, bl) = a, b
    lhs = cat([ah, al], 1)
    rhs = cat([cat([bh, bl], 1), cat([bh, jnp.zeros_like(bl)], 1)], 0)
    r = mm(lhs, rhs)
    return r[:, :C] + r[:, C:]


def wide3(a, b):
    (ah, al), (bh, bl) = a, b
    return mm(cat([ah, al], 1), cat([bh, bh], 0)) + mm(ah, bl)


def block_rows(ref, c):
    return cat([ref[hh][:, c * C : (c + 1) * C] for hh in range(ref.shape[0])], 0)


def tile(ref, hh, c):
    return ref[c * C : (c + 1) * C, hh * DH : (hh + 1) * DH]


def iotas():
    ri = lax.broadcasted_iota(jnp.int32, (C, C), 0)
    ci = lax.broadcasted_iota(jnp.int32, (C, C), 1)
    return ri, ci


def pair_list(hb, nc):
    return [(hh, c) for hh in range(hb) for c in range(nc)]


def log_sums(g_ref, pairs, ri, ci):
    triu = jnp.where(ri <= ci, 1.0, 0.0).astype(f32)
    rows = cat([g_ref[hh][:, c * C : (c + 1) * C] for hh, c in pairs], 0)
    return lax.dot_general(
        jnp.log(rows), triu, NN, precision=lax.Precision.HIGHEST, preferred_element_type=f32
    )


def map_kernel(k_ref, v_ref, g_ref, b_ref, uw_ref, s_ref, l_ref, pay_ref):
    rows = k_ref.shape[0]
    hb = g_ref.shape[0]
    nc = rows // C
    units = range(hb * nc)
    pairs = pair_list(hb, nc)
    ri, ci = iotas()
    eye = ri == ci
    xor = jnp.where(ri > ci, ri ^ ci, 0)
    identity = jnp.where(eye, 1.0, 0.0).astype(f32)

    logs = log_sums(g_ref, pairs, ri, ci)
    beta = cat([b_ref[hh][:, c * C : (c + 1) * C] for hh, c in pairs], 0)
    keys = [tile(k_ref, hh, c) for hh, c in pairs]
    grams = [mm(k, k, NT) for k in keys]
    diag = cat([jnp.sum(jnp.where(eye, g, 0.0), axis=0, keepdims=True) for g in grams], 0)
    key_scale = lax.rsqrt(diag * (1.0 / DH) + EPS) * (1.0 / math.sqrt(DH))
    growth = jnp.exp(logs)
    last = logs[:, C - 1 : C]
    decay = jnp.exp(last)
    tail = jnp.exp(last - logs) * key_scale
    bs = beta * key_scale
    logs_c, tail_c, bs_c, beta_c, bgs_c = (
        jnp.transpose(x) for x in (logs, tail, bs, beta, bs * growth)
    )
    for u, (hh, c) in enumerate(pairs):
        l_ref[hh, c] = jnp.broadcast_to(logs[u : u + 1], (8, C))
        l_ref[hh, nc + c] = jnp.broadcast_to(key_scale[u : u + 1], (8, C))

    negs, invs = [], []
    for u in units:
        col = slice(u, u + 1)
        ratio = jnp.exp(jnp.where(ri > ci, logs_c[:, col] - logs[col, :], NEG)) * key_scale[col, :]
        neg = grams[u] * ratio * (-bs_c[:, col])
        negs.append(split(neg))
        invs.append(identity + jnp.where(xor == 1, neg, 0.0))
    for level in range(1, C.bit_length() - 1):
        mask = (xor >> level) == 1
        parts = [split(t) for t in invs]
        left = [dot3(parts[u], negs[u]) for u in units]
        both = [dot3(split(left[u]), parts[u]) for u in units]
        invs = [invs[u] + jnp.where(mask, both[u], 0.0) for u in units]
    invs = [split(t) for t in invs]

    right = []
    for u, (hh, c) in enumerate(pairs):
        col = slice(u, u + 1)
        v = tile(v_ref, hh, c).astype(f32) * beta_c[:, col]
        k = keys[u].astype(f32) * bgs_c[:, col]
        right.append(split(cat([v, k], 1)))
    fixed = [wide3(invs[u], right[u]) for u in units]
    for u, (hh, c) in enumerate(pairs):
        uw_ref[hh, c] = fixed[u].astype(bf16)
    turned = [jnp.transpose(k) for k in keys]
    ends = [split(fixed[u] * tail_c[:, u : u + 1]) for u in units]
    maps = [mm(cat([turned[u], turned[u]], 1), cat(ends[u], 0)) for u in units]
    zero = jnp.zeros((C, DH), f32)
    start = cat([zero, identity], 1)

    states = []
    for hh in range(hb):
        u = hh * nc
        m = maps[u]
        states.append(cat([m[:, :DH], decay[u : u + 1, :] * identity - m[:, DH:]], 1))
    for c in range(1, nc):
        parts = [split(s) for s in states]
        for hh in range(hb):
            s_ref[hh, c - 1] = states[hh].astype(bf16)
        moved = [wide3(split(maps[hh * nc + c][:, DH:]), parts[hh]) for hh in range(hb)]
        for hh in range(hb):
            u = hh * nc + c
            offset = cat([maps[u][:, :DH], zero], 1)
            states[hh] = decay[u : u + 1, :] * states[hh] + (offset - moved[hh])

    row16 = lax.broadcasted_iota(jnp.int32, (16, DH), 0)
    for hh in range(hb):
        total = decay[hh * nc : hh * nc + 1, :]
        for c in range(1, nc):
            total = total * decay[hh * nc + c : hh * nc + c + 1, :]
        linear = (states[hh][:, DH:] - total * identity).astype(bf16)
        offset = jnp.transpose(states[hh][:, :DH]).astype(bf16)
        wide = jnp.broadcast_to(total, (16, DH))
        th = wide.astype(bf16).astype(f32)
        decays = jnp.where(row16 == 0, th, jnp.where(row16 == 1, wide - th, 0.0)).astype(bf16)
        for half in range(2):
            pay_ref[2 * hh + half, 0:128, :] = linear
            pay_ref[2 * hh + half, 128:192, :] = offset[half * 64 : (half + 1) * 64]
            pay_ref[2 * hh + half, 192:208, :] = decays


def out_kernel(q_ref, k_ref, uw_ref, l_ref, o_ref, y_ref):
    rows = q_ref.shape[0]
    hb = uw_ref.shape[0]
    nc = rows // C
    pairs = pair_list(hb, nc)
    ri, ci = iotas()
    lower = ri >= ci
    raw = [mm(tile(q_ref, hh, c), tile(k_ref, hh, c), NT) for hh, c in pairs]
    inner, growth = [], []
    for u, (hh, c) in enumerate(pairs):
        log_row, key_scale = l_ref[hh, c][0:1], l_ref[hh, nc + c][0:1]
        logs_c = jnp.transpose(l_ref[hh, c])[:, 0:1]
        mh, ml = split(raw[u] * (jnp.exp(jnp.where(lower, logs_c - log_row, NEG)) * key_scale))
        uw = uw_ref[hh, c]
        inner.append(mm(cat([mh, ml], 1), cat([uw, uw], 0)))
        growth.append(jnp.exp(logs_c))
    for u, (hh, c) in enumerate(pairs):
        qf = tile(q_ref, hh, c).astype(f32)
        scale = lax.rsqrt(jnp.mean(qf * qf, axis=1, keepdims=True) + EPS) * (1.0 / math.sqrt(DH))
        at = (slice(c * C, (c + 1) * C), slice(hh * DH, (hh + 1) * DH))
        o_ref[at] = inner[u][:, :DH] * scale
        y_ref[at] = ((growth[u] * qf - inner[u][:, DH:]) * scale).astype(bf16)


def chain_kernel(in_ref, out_ref):
    n = in_ref.shape[0]
    state = jnp.zeros((64, DH), f32)
    for j in range(n):
        out_ref[j] = state.astype(out_ref.dtype)
        if j == n - 1:
            break
        sh, sl = split(state)
        r = mm(cat([sh, sl], 0), in_ref[j, 0:128, :], NT)
        dec = in_ref[j, 192:208, :].astype(f32)
        total = dec[0:1] + dec[1:2]
        state = r[:64] + r[64:] + total * state + in_ref[j, 128:192, :].astype(f32)


def row_sums(acc_ref, at):
    return jnp.sum(jnp.transpose(acc_ref[at * DH : (at + 1) * DH, :]), axis=0, keepdims=True)


def attn_kernel(idx_ref, q_ref, k0_ref, v0_ref, kv1_ref, kv2_ref, prev_ref, o_ref, sq_ref, s_ref, QB=256):
    rows = q_ref.shape[0]
    hb = q_ref.shape[1] // DH
    nb = rows // QB
    ctx = idx_ref[0]
    scale = math.log2(math.e) / math.sqrt(DH)

    bias1 = jnp.where(ctx >= 1, 0.0, 1e30).astype(f32)
    bias2 = jnp.where(ctx >= 2, 0.0, 1e30).astype(f32)
    ri = lax.broadcasted_iota(jnp.int32, (QB, QB), 0)
    ci = lax.broadcasted_iota(jnp.int32, (QB, QB), 1)
    far = ci > ri

    @pl.when(pl.program_id(0) == 0)
    def _():
        s_ref[...] = jnp.zeros_like(s_ref)

    pairs = [(h, b) for h in range(hb) for b in range(nb)]

    def scores(h, b):
        lanes = slice(h * DH, (h + 1) * DH)
        q = q_ref[b * QB : (b + 1) * QB, lanes]
        s2 = mm(q, kv2_ref[0, b * QB :, lanes], NT)
        s1 = mm(q, kv1_ref[0, :, lanes], NT)
        s0 = mm(q, k0_ref[: (b + 1) * QB, lanes], NT)
        return s2, s1, s0

    def weights(b, s2, s1, s0):
        st = jnp.where(far, s2[:, :QB] - bias2, s0[:, b * QB :])
        parts = [(st, None), (s1, bias1)]
        if b < nb - 1:
            parts.append((s2[:, QB:], bias2))
        if b > 0:
            parts.append((s0[:, : b * QB], None))
        top = None
        for part, bias in parts:
            most = jnp.max(part, axis=1, keepdims=True)
            most = most if bias is None else most - bias
            top = most if top is None else jnp.maximum(top, most)
        raised = [jnp.exp2((p - (top if x is None else top + x)) * scale) for p, x in parts]
        total = sum(jnp.sum(p, axis=1, keepdims=True) for p in raised)
        w2 = jnp.where(far, raised[0], 0.0).astype(bf16)
        w0 = jnp.where(far, 0.0, raised[0]).astype(bf16)
        if b < nb - 1:
            w2 = cat([w2, raised[2].astype(bf16)], 1)
        if b > 0:
            w0 = cat([raised[-1].astype(bf16), w0], 1)
        return w2, raised[1].astype(bf16), w0, total

    def finish(h, b, w2, w1, w0, total):
        lanes = slice(h * DH, (h + 1) * DH)
        out = mm(w1, kv1_ref[1, :, lanes]) + mm(w2, kv2_ref[1, b * QB :, lanes]) + mm(w0, v0_ref[: (b + 1) * QB, lanes])
        out = out * (1.0 / total)
        o_ref[b * QB : (b + 1) * QB, lanes] = out
        s_ref[b * QB : (b + 1) * QB, :] += out * out

    ready = scores(*pairs[0])
    waiting = None
    for i, (h, b) in enumerate(pairs):
        current = ready
        if i + 1 < len(pairs):
            ready = scores(*pairs[i + 1])
        made = weights(b, *current)
        if waiting is not None:
            finish(*waiting)
        waiting = (h, b, *made)
    finish(*waiting)

    @pl.when(pl.program_id(0) == pl.num_programs(0) - 1)
    def _():
        n = rows // DH
        sums = cat([row_sums(s_ref, i) for i in range(n)] + [jnp.zeros((n, DH), f32)], 0)
        sq_ref[...] = prev_ref[...] + sums


def apply_kernel(o_ref, y_ref, m_ref, t_ref, prev_ref, d_ref, sq_ref, s_ref):
    rows = o_ref.shape[0]
    hb = m_ref.shape[0]
    nc = rows // C

    @pl.when(pl.program_id(0) == 0)
    def _():
        s_ref[...] = jnp.zeros_like(s_ref)

    firsts = [cat([t_ref[2 * hh], t_ref[2 * hh + 1]], 0) for hh in range(hb)]
    pairs = [(hh, c) for c in range(1, nc) for hh in range(hb)]
    states = [
        m_ref[hh, c - 1][:, :DH].astype(f32) + mm(m_ref[hh, c - 1][:, DH:], firsts[hh], NT) for hh, c in pairs
    ]
    states = [split(x) for x in states]
    outs = {}
    for hh in range(hb):
        outs[hh, 0] = mm(tile(y_ref, hh, 0), firsts[hh], NT)
    for (hh, c), state in zip(pairs, states):
        y = tile(y_ref, hh, c)
        outs[hh, c] = mm(cat([y, y], 1), cat(state, 0))
    for (hh, c), moved in outs.items():
        out = tile(o_ref, hh, c) + moved
        at = slice(c * C, (c + 1) * C)
        d_ref[at, hh * DH : (hh + 1) * DH] = out
        s_ref[at, :] += out * out

    @pl.when(pl.program_id(0) == pl.num_programs(0) - 1)
    def _():
        n = rows // DH
        sums = cat([jnp.zeros((n, DH), f32)] + [row_sums(s_ref, i) for i in range(n)], 0)
        sq_ref[...] = prev_ref[...] + sums


def join_kernel(sq_ref, *refs):
    a_refs, (d_ref, ag_ref, dg_ref, o_ref) = refs[:-4], refs[-4:]
    n = sq_ref.shape[0] // 2
    scales = jnp.transpose(0.5 * lax.rsqrt(sq_ref[...] * (1.0 / WIDTH) + EPS))
    lane = lax.broadcasted_iota(jnp.int32, scales.shape, 1)
    i = pl.program_id(0)
    attn_scale = jnp.sum(jnp.where(lane == i, scales, 0.0), axis=1, keepdims=True)
    delta_scale = jnp.sum(jnp.where(lane == i + n, scales, 0.0), axis=1, keepdims=True)
    at = 0
    for a_ref in a_refs:
        lanes = slice(at, at + a_ref.shape[1])
        at += a_ref.shape[1]
        o_ref[:, lanes] = (
            ag_ref[:, lanes] * a_ref[...] * attn_scale + dg_ref[:, lanes] * d_ref[:, lanes] * delta_scale
        ).astype(bf16)


def params():
    return pltpu.CompilerParams(vmem_limit_bytes=60 * 2**20)


def cost(us):
    return pl.CostEstimate(flops=int(us * 1e9), bytes_accessed=0, transcendentals=0)


def on_device(aq, ak, av, dq, dk, dv, gate, beta, ag, dg):
    rows, width = aq.shape
    heads = gate.shape[1]
    nctx = lax.axis_size("ctx")
    nc = rows // C
    index = lax.axis_index("ctx").astype(jnp.int32).reshape(1)

    hop = [(i, i + 2) for i in range(nctx - 2)]
    swap = [(i, i + 1 - 2 * (i % 2)) for i in range(nctx)]
    odd = index[0] % 2 == 1

    def send(x, pairs):
        return lax.ppermute(x, "ctx", pairs)

    parts, at = [], 0
    for count in PARTS:
        parts.append((at * DH, count * DH))
        at += count
    own = [jnp.stack([x[:, at : at + size] for x in (ak, av)]) for at, size in parts]
    two = [send(x, hop) for x in own]

    gt = gate.T.reshape(heads, 1, rows)
    bt = beta.T.reshape(heads, 1, rows)

    def wide(hb):
        return pl.BlockSpec((rows, hb * DH), lambda h: (0, h))

    def lead(*shape):
        return pl.BlockSpec(shape, lambda h: (h,) + (0,) * (len(shape) - 1))

    def shaped(shape, dtype=f32):
        return jax.ShapeDtypeStruct(shape, dtype)

    hb = 4
    fixed, maps, logs, pay = pl.pallas_call(
        map_kernel,
        grid=(heads // hb,),
        in_specs=[wide(hb), wide(hb), lead(hb, 1, rows), lead(hb, 1, rows)],
        out_specs=[lead(hb, nc, C, 2 * DH), lead(hb, nc - 1, DH, 2 * DH), lead(hb, 2 * nc, 8, C), lead(2 * hb, PAY, DH)],
        out_shape=[
            shaped((heads, nc, C, 2 * DH), bf16),
            shaped((heads, nc - 1, DH, 2 * DH), bf16),
            shaped((heads, 2 * nc, 8, C)),
            shaped((nctx, PAY, DH), bf16),
        ],
        compiler_params=params(),
        cost_estimate=cost(COSTS[0]),
        name="delta_maps",
    )(dk, dv, gt, bt)

    got = lax.all_to_all(pay, "ctx", 0, 0, tiled=True)

    hb = 3
    local, effect = pl.pallas_call(
        out_kernel,
        grid=(heads // hb,),
        in_specs=[wide(hb), wide(hb), lead(hb, nc, C, 2 * DH), lead(hb, 2 * nc, 8, C)],
        out_specs=[wide(hb), wide(hb)],
        out_shape=[shaped((rows, width)), shaped((rows, width), bf16)],
        compiler_params=params(),
        cost_estimate=cost(COSTS[1]),
        name="delta_rows",
    )(dq, dk, fixed, logs)

    def before(i, token):
        two[i], token = lax.optimization_barrier((two[i], token))
        return send(jnp.where(odd, two[i], own[i]), swap), token

    one = [None] * len(parts)
    one[0], local = before(0, local)

    chain = pl.pallas_call(
        chain_kernel,
        out_shape=shaped((nctx, 64, DH), bf16),
        compiler_params=params(),
        cost_estimate=cost(COSTS[2]),
        name="delta_chain",
    )(got)

    whole = pl.BlockSpec((2 * rows // DH, DH), lambda h: (0, 0))
    hb = AH

    def attend(i, prev):
        steps = parts[i][1] // (hb * DH)
        first = parts[i][0] // (hb * DH)
        mine = pl.BlockSpec((rows, hb * DH), lambda h: (0, first + h))
        both = pl.BlockSpec((2, rows, hb * DH), lambda h: (0, 0, h))
        return pl.pallas_call(
            functools.partial(attn_kernel, QB=QB),
            grid=(steps,),
            in_specs=[pl.BlockSpec(memory_space=pltpu.SMEM), mine, mine, mine, both, both, whole],
            out_specs=[wide(hb), whole],
            out_shape=[shaped((rows, parts[i][1])), shaped((2 * rows // DH, DH))],
            scratch_shapes=[pltpu.VMEM((rows, DH), f32)],
            compiler_params=params(),
            cost_estimate=cost(COSTS[3]),
            name=f"window_attention_{i}",
        )(index, aq, ak, av, one[i], two[i], prev)

    squares = jnp.zeros((2 * rows // DH, DH), f32)
    squares, chain = lax.optimization_barrier((squares, chain))
    states = lax.all_to_all(chain, "ctx", 0, 0, tiled=True)
    attn = []
    out, squares = attend(0, squares)
    attn.append(out)
    one[1], squares = before(1, squares)

    hb = 2
    delta, squares = pl.pallas_call(
        apply_kernel,
        grid=(heads // hb,),
        in_specs=[wide(hb), wide(hb), lead(hb, nc - 1, DH, 2 * DH), lead(2 * hb, 64, DH), whole],
        out_specs=[wide(hb), whole],
        out_shape=[shaped((rows, width)), shaped((2 * rows // DH, DH))],
        scratch_shapes=[pltpu.VMEM((rows, DH), f32)],
        compiler_params=params(),
        cost_estimate=cost(COSTS[4]),
        name="delta_apply",
    )(local, effect, maps, states, squares)

    one[2], squares = before(2, squares)
    for i in range(1, len(parts)):
        out, squares = attend(i, squares)
        attn.append(out)
    squares = lax.psum(squares, "head")

    cols = pl.BlockSpec((DH, width), lambda i: (i, 0))
    gains = pl.BlockSpec((1, width), lambda i: (0, 0))
    return pl.pallas_call(
        join_kernel,
        grid=(rows // DH,),
        in_specs=[whole] + [pl.BlockSpec((DH, size), lambda i: (i, 0)) for _, size in parts] + [cols, gains, gains],
        out_specs=cols,
        out_shape=shaped((rows, width), bf16),
        compiler_params=params(),
        name="join",
    )(squares, *attn, delta, ag.reshape(1, width), dg.reshape(1, width))


def solution(mesh):
    shard = P("ctx", "head")
    return jax.shard_map(
        on_device,
        mesh=mesh,
        in_specs=(shard,) * 8 + (P("head"), P("head")),
        out_specs=shard,
        check_vma=False,
    )
```

time: 258 us -> 163 us (0.63)
  the two profiles are of different devices: /device:TPU:84 before, /device:TPU:6 now
where the time goes in v1:
time: 163 us; the launch traced here: 162 us
  Pallas kernels  67.4 us (41%)
  waiting for transfers between devices  37 us (23%)
  starting transfers between devices  36.1 us (22%)
  local copies, waits for them, and re-layouts  9.68 us (6%)
  blocking collectives  8.08 us (5%)
  other arithmetic  4.04 us (2%)
    ppermute x6, waiting for transfers between devices, send(): return lax.ppermute(x, 'ctx', pairs)  37 us
    pallas_call x1, Pallas kernels, on_device(): pl.pallas_call(map_kernel, grid=(heads // hb,), in_specs=[wide(hb), wide(...  21.8 us
    pallas_call x3, Pallas kernels, attend(): pl.pallas_call(functools.partial(attn_kernel, QB=QB), grid=(steps,), in_s...  19.2 us
    ppermute x6, starting transfers between devices, send(): return lax.ppermute(x, 'ctx', pairs)  15.9 us
    all_to_all x1, starting transfers between devices, on_device(): states = lax.all_to_all(chain, 'ctx', 0, 0, tiled=True)  11.2 us
    all_to_all x1, starting transfers between devices, on_device(): got = lax.all_to_all(pay, 'ctx', 0, 0, tiled=True)  9.01 us
    psum x1, blocking collectives, on_device(): squares = lax.psum(squares, 'head')  8.08 us
    pallas_call x1, Pallas kernels, on_device(): pl.pallas_call(out_kernel, grid=(heads // hb,), in_specs=[wide(hb), wide(...  7.76 us
  transfers between devices with their start and end apart: 8, of which 5 were waited for; matrix products, arithmetic and copies ran while one was open for 5% of the time, Pallas kernels for 36%

profile of v1, /device:TPU:6, one launch (start us, length us, event | category | flops | bytes accessed | tf_op | source)
XLA Modules:
  0.0 162.4 jit_solution(4506127907186237669)
XLA Ops:
  0.0 1.5 slice_bitcast_fusion
  1.5 0.0 copy-start.3
  1.5 0.0 copy-start.4
  1.5 1.3 pad_maximum_fusion
  2.8 3.8 %collective-permute-start.1 = (bf16[2,512,768]{2,1,0:T(8,128)(2,1)}, bf16[2,512,768]{2,1,0:T(8,128)(2,1)}, u32[]{:S(2)}, u32[]{:S(2)}) collective-permute-start(bf16[2,512,768]{2,1,0:T(8,128)(2,1)} %pad_maximum_fusion), channel_id=1, source_target_pairs={{0,8},{4,12},{8,16},{12,20},{16,24},{20,28},{24,32},{28,36},{32,40... | collective-permute-start | bytes 4718600 | tf_op jit(solution)/shard_map/ppermute | solution.py:361
  6.6 0.0 copy-done.3
  6.6 0.6 reshape.16.g_ref
  7.3 0.0 copy-done.4
  7.3 0.6 reshape.17.b_ref
  7.9 21.8 %delta_maps.1 = (bf16[12,4,128,256]{3,2,1,0:T(8,128)(2,1)}, bf16[12,3,128,256]{3,2,1,0:T(8,128)(2,1)}, f32[12,8,8,128]{3,2,1,0:T(8,128)}, bf16[32,208,128]{2,1,0:T(8,128)(2,1)}) custom-call(bf16[512,1536]{1,0:T(8,128)(2,1)} %k_ref.3, bf16[512,1536]{1,0:T(8,128)(2,1)} %v_ref.1, f32[12,1,512]{2,1,0:T(1,128)} %reshape.16.g_ref, f32[12,1,512]{2,1,0:T(1,128)} %reshape.17.b_ref), custom_call_target="tpu_custom_call" | custom-call | flops 2000000000 | tf_op jit(solution)/shard_map/delta_maps/pallas_call | solution.py:383
  29.7 9.0 %all-to-all-start = ((bf16[32,208,128]{2,1,0:T(8,128)(2,1)}), bf16[32,208,128]{2,1,0:T(8,128)(2,1)S(1)}, u32[]{:S(2)}, u32[]{:S(2)}) async-start(bf16[32,208,128]{2,1,0:T(8,128)(2,1)} %get-tuple-element.33), calls=%async_computation | async-start | bytes 3407872 | tf_op jit(solution)/shard_map/all_to_all | solution.py:399
  38.7 7.8 %delta_rows.1 = (f32[512,1536]{1,0:T(8,128)}, bf16[512,1536]{1,0:T(8,128)(2,1)}) custom-call(bf16[512,1536]{1,0:T(8,128)(2,1)} %q_ref.4, bf16[512,1536]{1,0:T(8,128)(2,1)} %k_ref.3, bf16[12,4,128,256]{3,2,1,0:T(8,128)(2,1)} %get-tuple-element.27.uw_ref, f32[12,8,8,128]{3,2,1,0:T(8,128)} %get-tuple-element.28.l_ref), custom_call_target="tpu_custom_call" | custom-call | flops 8000000000 | tf_op jit(solution)/shard_map/delta_rows/pallas_call | solution.py:402
  46.5 10.1 %collective-permute-done.1.kv2_ref = bf16[2,512,768]{2,1,0:T(8,128)(2,1)} collective-permute-done((bf16[2,512,768]{2,1,0:T(8,128)(2,1)}, bf16[2,512,768]{2,1,0:T(8,128)(2,1)}, u32[]{:S(2)}, u32[]{:S(2)}) %collective-permute-start.1) | collective-permute-done | bytes 1572896 | tf_op jit(solution)/shard_map/ppermute | solution.py:361
  56.6 1.4 broadcast_select_fusion
  57.9 0.0 collective-permute-start.3
  57.9 1.3 slice_bitcast_fusion.2
  59.2 1.1 pad_maximum_fusion.1
  60.3 5.3 %collective-permute-start.2 = (bf16[2,512,512]{2,1,0:T(8,128)(2,1)}, bf16[2,512,512]{2,1,0:T(8,128)(2,1)}, u32[]{:S(2)}, u32[]{:S(2)}) collective-permute-start(bf16[2,512,512]{2,1,0:T(8,128)(2,1)} %pad_maximum_fusion.1), channel_id=1, source_target_pairs={{0,8},{4,12},{8,16},{12,20},{16,24},{20,28},{24,32},{28,36},{32,40... | collective-permute-start | bytes 3145736 | tf_op jit(solution)/shard_map/ppermute | solution.py:361
  65.6 0.0 all-to-all-done.in_ref
  65.6 0.0 copy-start
  65.6 1.2 copy-done
  66.8 6.3 %delta_chain.1 = bf16[32,64,128]{2,1,0:T(8,128)(2,1)} custom-call(bf16[32,208,128]{2,1,0:T(8,128)(2,1)} %copy-done), custom_call_target="tpu_custom_call" | custom-call | flops 5000000000 | tf_op jit(solution)/shard_map/delta_chain/pallas_call | solution.py:420
  73.1 11.2 %all-to-all-start.1 = ((bf16[32,64,128]{2,1,0:T(8,128)(2,1)}), bf16[32,64,128]{2,1,0:T(8,128)(2,1)S(1)}, u32[]{:S(2)}, u32[]{:S(2)}) async-start(bf16[32,64,128]{2,1,0:T(8,128)(2,1)} %delta_chain.1), calls=%async_computation.1 | async-start | bytes 1048576 | tf_op jit(solution)/shard_map/all_to_all | solution.py:450
  84.3 13.9 %collective-permute-done.3.kv1_ref = bf16[2,512,768]{2,1,0:T(8,128)(2,1)} collective-permute-done((bf16[2,512,768]{2,1,0:T(8,128)(2,1)}, bf16[2,512,768]{2,1,0:T(8,128)(2,1)}, u32[]{:S(2)}, u32[]{:S(2)}) %collective-permute-start.3) | collective-permute-done | bytes 1572896 | tf_op jit(solution)/shard_map/ppermute | solution.py:361
  98.2 0.6 broadcast_in_dim.3.prev_ref
  98.7 8.5 %window_attention_0.1 = (f32[512,768]{1,0:T(8,128)}, f32[8,128]{1,0:T(8,128)}) custom-call(s32[1]{0:T(128)} %bitcast.idx_ref, bf16[512,1536]{1,0:T(8,128)(2,1)} %q_ref.7, bf16[512,1536]{1,0:T(8,128)(2,1)} %k0_ref.5, bf16[512,1536]{1,0:T(8,128)(2,1)} %v0_ref.5, bf16[2,512,768]{2,1,0:T(8,128)(2,1)} %collective-permute-done.3.kv1_ref, ...), custom_call_target="tpu_custom_call" | custom-call | flops 10000000000 | tf_op jit(solution)/shard_map/window_attention_0/pallas_call | solution.py:436
  107.2 0.0 collective-permute-done.2.kv2_ref
  107.2 0.1 broadcast_select_fusion.1
  107.4 0.0 copy-start.5
  107.4 0.0 copy-start.6
  107.4 3.0 %collective-permute-start.5 = (bf16[2,512,512]{2,1,0:T(8,128)(2,1)S(1)}, bf16[2,512,512]{2,1,0:T(8,128)(2,1)}, u32[]{:S(2)}, u32[]{:S(2)}) collective-permute-start(bf16[2,512,512]{2,1,0:T(8,128)(2,1)S(1)} %broadcast_select_fusion.1), channel_id=1, source_target_pairs={{0,4},{4,0},{8,12},{12,8},{16,20},{20,16},{24,28},{28,24},{32,36},... | collective-permute-start | bytes 3145736 | tf_op jit(solution)/shard_map/ppermute | solution.py:361
  110.4 1.1 slice_bitcast_fusion.4
  111.4 0.1 pad_maximum_fusion.2
  111.5 3.4 %collective-permute-start = (bf16[2,512,256]{2,1,0:T(8,128)(2,1)S(1)}, bf16[2,512,256]{2,1,0:T(8,128)(2,1)S(1)}, u32[]{:S(2)}, u32[]{:S(2)}) collective-permute-start(bf16[2,512,256]{2,1,0:T(8,128)(2,1)S(1)} %pad_maximum_fusion.2), channel_id=1, source_target_pairs={{0,8},{4,12},{8,16},{12,20},{16,24},{20,28},{24,32},{28,36},{32,40... | collective-permute-start | bytes 1572872 | tf_op jit(solution)/shard_map/ppermute | solution.py:361
  114.9 0.0 copy-done.5
  114.9 0.6 reshape.18.refs_4_
  115.5 0.0 copy-done.6
  115.5 0.6 reshape.19.refs_5_
  116.1 0.0 all-to-all-done.1.t_ref
  116.1 0.0 copy-start.1
  116.1 0.8 copy-done.1
  117.0 7.4 %delta_apply.1 = (f32[512,1536]{1,0:T(8,128)}, f32[8,128]{1,0:T(8,128)}) custom-call(f32[512,1536]{1,0:T(8,128)} %get-tuple-element.30.o_ref, bf16[512,1536]{1,0:T(8,128)(2,1)} %get-tuple-element.31.y_ref, bf16[12,3,128,256]{3,2,1,0:T(8,128)(2,1)} %get-tuple-element.32.m_ref, bf16[32,64,128]{2,1,0:T(8,128)(2,1)} %copy-done.1, ...), custom_call_target="tpu_custom_call" | custom-call | flops 5000000000 | tf_op jit(solution)/shard_map/delta_apply/pallas_call | solution.py:457
  124.3 4.2 %collective-permute-done.kv2_ref = bf16[2,512,256]{2,1,0:T(8,128)(2,1)S(1)} collective-permute-done((bf16[2,512,256]{2,1,0:T(8,128)(2,1)S(1)}, bf16[2,512,256]{2,1,0:T(8,128)(2,1)S(1)}, u32[]{:S(2)}, u32[]{:S(2)}) %collective-permute-start) | collective-permute-done | bytes 524320 | tf_op jit(solution)/shard_map/ppermute | solution.py:361
  128.5 0.0 copy-start.2
  128.5 0.1 broadcast_select_fusion.2
  128.6 0.4 collective-permute-start.4
  129.0 5.5 %collective-permute-done.5.kv1_ref = bf16[2,512,512]{2,1,0:T(8,128)(2,1)} collective-permute-done((bf16[2,512,512]{2,1,0:T(8,128)(2,1)S(1)}, bf16[2,512,512]{2,1,0:T(8,128)(2,1)}, u32[]{:S(2)}, u32[]{:S(2)}) %collective-permute-start.5) | collective-permute-done | bytes 1048608 | tf_op jit(solution)/shard_map/ppermute | solution.py:361
  134.5 6.6 %window_attention_1.1 = (f32[512,512]{1,0:T(8,128)}, f32[8,128]{1,0:T(8,128)}) custom-call(s32[1]{0:T(128)} %bitcast.idx_ref, bf16[512,1536]{1,0:T(8,128)(2,1)} %q_ref.7, bf16[512,1536]{1,0:T(8,128)(2,1)} %k0_ref.5, bf16[512,1536]{1,0:T(8,128)(2,1)} %v0_ref.5, bf16[2,512,512]{2,1,0:T(8,128)(2,1)} %collective-permute-done.5.kv1_ref, ...), custom_call_target="tpu_custom_call" | custom-call | flops 10000000000 | tf_op jit(solution)/shard_map/window_attention_1/pallas_call | solution.py:436
  141.1 0.0 copy-done.2
  141.1 3.4 %collective-permute-done.4.kv1_ref = bf16[2,512,256]{2,1,0:T(8,128)(2,1)S(1)} collective-permute-done((bf16[2,512,256]{2,1,0:T(8,128)(2,1)S(1)}, bf16[2,512,256]{2,1,0:T(8,128)(2,1)S(1)}, u32[]{:S(2)}, u32[]{:S(2)}) %collective-permute-start.4) | collective-permute-done | bytes 524320 | tf_op jit(solution)/shard_map/ppermute | solution.py:361
  144.4 0.0 copy-start.7
  144.4 0.8 copy-done.7
  145.2 4.2 %window_attention_2.1 = (f32[512,256]{1,0:T(8,128)}, f32[8,128]{1,0:T(8,128)}) custom-call(s32[1]{0:T(128)} %bitcast.idx_ref, bf16[512,1536]{1,0:T(8,128)(2,1)} %q_ref.7, bf16[512,1536]{1,0:T(8,128)(2,1)} %k0_ref.5, bf16[512,1536]{1,0:T(8,128)(2,1)} %v0_ref.5, bf16[2,512,256]{2,1,0:T(8,128)(2,1)} %copy-done.7, bf16[2,512,256]{2,1,0:T(8,128)(2,1)} %copy-done.2, ...), custom_call_target="tpu_custom_call" | custom-call | flops 10000000000 | tf_op jit(solution)/shard_map/window_attention_2/pallas_call | solution.py:436
  149.4 8.1 %psum.7.sq_ref = f32[8,128]{1,0:T(8,128)} all-reduce(f32[8,128]{1,0:T(8,128)} %get-tuple-element.44), channel_id=1, replica_groups=mesh['ctx'=32,'head'=4] {'head'}, use_global_device_ids=true, to_apply=%region_0.1 | all-reduce | flops 1024 | bytes 8192 | tf_op jit(solution)/shard_map/psum | solution.py:473
  157.5 4.9 %join.1 = bf16[512,1536]{1,0:T(8,128)(2,1)} custom-call(f32[8,128]{1,0:T(8,128)} %psum.7.sq_ref, f32[512,768]{1,0:T(8,128)} %get-tuple-element.45.refs_0_, f32[512,512]{1,0:T(8,128)} %get-tuple-element.46.refs_1_, f32[512,256]{1,0:T(8,128)} %get-tuple-element.47.refs_2_, f32[512,1536]{1,0:T(8,128)} %get-tuple-element.48.refs_3_, f32[1,1536]{1,0:T(1,128)} %reshape.18.refs_4_, ...), custom_call_target="tpu_custom_call" | custom-call | tf_op jit(solution)/shard_map/join/pallas_call | solution.py:477
Async XLA Ops:
  1.5 5.2 %copy-start.3 = (f32[512,12]{0,1:T(8,128)S(1)}, f32[512,12]{0,1:T(8,128)}, u32[]{:S(2)}) copy-start(f32[512,12]{0,1:T(8,128)} %param.16) | copy-start | bytes 73732
  1.5 5.8 %copy-start.4 = (f32[512,12]{0,1:T(8,128)S(1)}, f32[512,12]{0,1:T(8,128)}, u32[]{:S(2)}) copy-start(f32[512,12]{0,1:T(8,128)} %param.17) | copy-start | bytes 73732
  2.8 53.8 %collective-permute-start.1 = (bf16[2,512,768]{2,1,0:T(8,128)(2,1)}, bf16[2,512,768]{2,1,0:T(8,128)(2,1)}, u32[]{:S(2)}, u32[]{:S(2)}) collective-permute-start(bf16[2,512,768]{2,1,0:T(8,128)(2,1)} %pad_maximum_fusion), channel_id=1, source_target_pairs={{0,8},{4,12},{8,16},{12,20},{16,24},{20,28},{24,32},{28,36},{32,40... | collective-permute-start | bytes 4718600 | tf_op jit(solution)/shard_map/ppermute | solution.py:361
  29.7 35.9 %all-to-all-start = ((bf16[32,208,128]{2,1,0:T(8,128)(2,1)}), bf16[32,208,128]{2,1,0:T(8,128)(2,1)S(1)}, u32[]{:S(2)}, u32[]{:S(2)}) async-start(bf16[32,208,128]{2,1,0:T(8,128)(2,1)} %get-tuple-element.33), calls=%async_computation | async-start | bytes 3407872 | tf_op jit(solution)/shard_map/all_to_all | solution.py:399
  57.9 40.2 %collective-permute-start.3 = (bf16[2,512,768]{2,1,0:T(8,128)(2,1)}, bf16[2,512,768]{2,1,0:T(8,128)(2,1)}, u32[]{:S(2)}, u32[]{:S(2)}) collective-permute-start(bf16[2,512,768]{2,1,0:T(8,128)(2,1)} %broadcast_select_fusion), channel_id=1, source_target_pairs={{0,4},{4,0},{8,12},{12,8},{16,20},{20,16},{24,28},{28,24},{32,36},... | collective-permute-start | bytes 4718600 | tf_op jit(solution)/shard_map/ppermute | solution.py:361
  60.3 46.9 %collective-permute-start.2 = (bf16[2,512,512]{2,1,0:T(8,128)(2,1)}, bf16[2,512,512]{2,1,0:T(8,128)(2,1)}, u32[]{:S(2)}, u32[]{:S(2)}) collective-permute-start(bf16[2,512,512]{2,1,0:T(8,128)(2,1)} %pad_maximum_fusion.1), channel_id=1, source_target_pairs={{0,8},{4,12},{8,16},{12,20},{16,24},{20,28},{24,32},{28,36},{32,40... | collective-permute-start | bytes 3145736 | tf_op jit(solution)/shard_map/ppermute | solution.py:361
  65.6 1.2 copy-start
  73.1 43.0 %all-to-all-start.1 = ((bf16[32,64,128]{2,1,0:T(8,128)(2,1)}), bf16[32,64,128]{2,1,0:T(8,128)(2,1)S(1)}, u32[]{:S(2)}, u32[]{:S(2)}) async-start(bf16[32,64,128]{2,1,0:T(8,128)(2,1)} %delta_chain.1), calls=%async_computation.1 | async-start | bytes 1048576 | tf_op jit(solution)/shard_map/all_to_all | solution.py:450
  107.4 7.5 %copy-start.5 = (f32[1536]{0:T(1024)S(1)}, f32[1536]{0:T(1024)}, u32[]{:S(2)}) copy-start(f32[1536]{0:T(1024)} %param.18) | copy-start | bytes 18436
  107.4 8.1 %copy-start.6 = (f32[1536]{0:T(1024)S(1)}, f32[1536]{0:T(1024)}, u32[]{:S(2)}) copy-start(f32[1536]{0:T(1024)} %param.19) | copy-start | bytes 18436
  107.4 27.1 %collective-permute-start.5 = (bf16[2,512,512]{2,1,0:T(8,128)(2,1)S(1)}, bf16[2,512,512]{2,1,0:T(8,128)(2,1)}, u32[]{:S(2)}, u32[]{:S(2)}) collective-permute-start(bf16[2,512,512]{2,1,0:T(8,128)(2,1)S(1)} %broadcast_select_fusion.1), channel_id=1, source_target_pairs={{0,4},{4,0},{8,12},{12,8},{16,20},{20,16},{24,28},{28,24},{32,36},... | collective-permute-start | bytes 3145736 | tf_op jit(solution)/shard_map/ppermute | solution.py:361
  111.5 17.1 %collective-permute-start = (bf16[2,512,256]{2,1,0:T(8,128)(2,1)S(1)}, bf16[2,512,256]{2,1,0:T(8,128)(2,1)S(1)}, u32[]{:S(2)}, u32[]{:S(2)}) collective-permute-start(bf16[2,512,256]{2,1,0:T(8,128)(2,1)S(1)} %pad_maximum_fusion.2), channel_id=1, source_target_pairs={{0,8},{4,12},{8,16},{12,20},{16,24},{20,28},{24,32},{28,36},{32,40... | collective-permute-start | bytes 1572872 | tf_op jit(solution)/shard_map/ppermute | solution.py:361
  116.1 0.8 copy-start.1
  128.5 12.5 %copy-start.2 = (bf16[2,512,256]{2,1,0:T(8,128)(2,1)}, bf16[2,512,256]{2,1,0:T(8,128)(2,1)S(1)}, u32[]{:S(2)}) copy-start(bf16[2,512,256]{2,1,0:T(8,128)(2,1)S(1)} %collective-permute-done.kv2_ref) | copy-start | bytes 1572868
  128.6 15.8 %collective-permute-start.4 = (bf16[2,512,256]{2,1,0:T(8,128)(2,1)S(1)}, bf16[2,512,256]{2,1,0:T(8,128)(2,1)S(1)}, u32[]{:S(2)}, u32[]{:S(2)}) collective-permute-start(bf16[2,512,256]{2,1,0:T(8,128)(2,1)S(1)} %broadcast_select_fusion.2), channel_id=1, source_target_pairs={{0,4},{4,0},{8,12},{12,8},{16,20},{20,16},{24,28},{28,24},{32,36},... | collective-permute-start | bytes 1572872 | tf_op jit(solution)/shard_map/ppermute | solution.py:361
  144.4 0.8 copy-start.7

commit v2 on v1

--- a/solution.py
+++ b/solution.py
@@ -16,7 +16,7 @@
 PARTS = (6, 4, 2)
 AH = 2
 QB = 256
-COSTS = (2, 8, 5, 10, 5)
+COSTS = (2, 8, 5, 1, 5)
 PAY = 208
 NEG = -1e30
 f32 = jnp.float32
@@ -449,9 +449,12 @@
     squares, chain = lax.optimization_barrier((squares, chain))
     states = lax.all_to_all(chain, "ctx", 0, 0, tiled=True)
     attn = []
+    one[1], squares = before(1, squares)
     out, squares = attend(0, squares)
     attn.append(out)
-    one[1], squares = before(1, squares)
+    one[2], squares = before(2, squares)
+    out, squares = attend(1, squares)
+    attn.append(out)
 
     hb = 2
     delta, squares = pl.pallas_call(
@@ -466,10 +469,8 @@
         name="delta_apply",
     )(local, effect, maps, states, squares)
 
-    one[2], squares = before(2, squares)
-    for i in range(1, len(parts)):
-        out, squares = attend(i, squares)
-        attn.append(out)
+    out, squares = attend(2, squares)
+    attn.append(out)
     squares = lax.psum(squares, "head")
 
     cols = pl.BlockSpec((DH, width), lambda i: (i, 0))

time: 163 us -> 160 us (0.982)
  the two profiles are of different devices: /device:TPU:6 before, /device:TPU:84 now
where the time goes in v2:
time: 160 us; the launch traced here: 159 us
  Pallas kernels  67.7 us (42%)
  waiting for transfers between devices  37.2 us (23%)
  starting transfers between devices  31 us (19%)
  local copies, waits for them, and re-layouts  7.92 us (5%)
  blocking collectives  7.83 us (5%)
  other arithmetic  7.56 us (5%)
    ppermute x6, waiting for transfers between devices, send(): return lax.ppermute(x, 'ctx', pairs)  37.2 us
    pallas_call x1, Pallas kernels, on_device(): pl.pallas_call(map_kernel, grid=(heads // hb,), in_specs=[wide(hb), wide(...  21.8 us
    pallas_call x3, Pallas kernels, attend(): pl.pallas_call(functools.partial(attn_kernel, QB=QB), grid=(steps,), in_s...  19.4 us
    ppermute x6, starting transfers between devices, send(): return lax.ppermute(x, 'ctx', pairs)  13.6 us
    all_to_all x1, starting transfers between devices, on_device(): states = lax.all_to_all(chain, 'ctx', 0, 0, tiled=True)  9.04 us
    all_to_all x1, starting transfers between devices, on_device(): got = lax.all_to_all(pay, 'ctx', 0, 0, tiled=True)  8.42 us
    psum x1, blocking collectives, on_device(): squares = lax.psum(squares, 'head')  7.83 us
    pallas_call x1, Pallas kernels, on_device(): pl.pallas_call(out_kernel, grid=(heads // hb,), in_specs=[wide(hb), wide(...  7.76 us
  transfers between devices with their start and end apart: 8, of which 3 were waited for; matrix products, arithmetic and copies ran while one was open for 6% of the time, Pallas kernels for 37%

profile of v2, /device:TPU:84, one launch (start us, length us, event | category | flops | bytes accessed | tf_op | source)
XLA Modules:
  0.0 159.5 jit_solution(6332688361728366287)
XLA Ops:
  0.0 1.5 slice_bitcast_fusion
  1.5 0.0 copy-start.2
  1.5 0.0 copy-start.3
  1.5 0.0 copy-start.12
  1.5 0.0 copy-start.13
  1.5 1.4 pad_maximum_fusion
  2.9 0.0 copy-done.2
  2.9 0.2 copy-done.3
  3.1 3.5 %collective-permute-start.1 = (bf16[2,512,768]{2,1,0:T(8,128)(2,1)}, bf16[2,512,768]{2,1,0:T(8,128)(2,1)}, u32[]{:S(2)}, u32[]{:S(2)}) collective-permute-start(bf16[2,512,768]{2,1,0:T(8,128)(2,1)} %pad_maximum_fusion), channel_id=1, source_target_pairs={{0,8},{4,12},{8,16},{12,20},{16,24},{20,28},{24,32},{28,36},{32,40... | collective-permute-start | bytes 4718600 | tf_op jit(solution)/shard_map/ppermute | solution.py:361
  6.7 0.0 copy-done.12
  6.7 0.6 reshape.16.g_ref
  7.3 0.0 copy-done.13
  7.3 0.6 reshape.17.b_ref
  7.9 21.8 %delta_maps.1 = (bf16[12,4,128,256]{3,2,1,0:T(8,128)(2,1)}, bf16[12,3,128,256]{3,2,1,0:T(8,128)(2,1)}, f32[12,8,8,128]{3,2,1,0:T(8,128)}, bf16[32,208,128]{2,1,0:T(8,128)(2,1)}) custom-call(bf16[512,1536]{1,0:T(8,128)(2,1)} %k_ref.3, bf16[512,1536]{1,0:T(8,128)(2,1)} %v_ref.1, f32[12,1,512]{2,1,0:T(1,128)} %reshape.16.g_ref, f32[12,1,512]{2,1,0:T(1,128)} %reshape.17.b_ref), custom_call_target="tpu_custom_call" | custom-call | flops 2000000000 | tf_op jit(solution)/shard_map/delta_maps/pallas_call | solution.py:383
  29.8 0.0 copy-start
  29.8 0.0 copy-start.1
  29.8 8.4 %all-to-all-start = ((bf16[32,208,128]{2,1,0:T(8,128)(2,1)}), bf16[32,208,128]{2,1,0:T(8,128)(2,1)}, u32[]{:S(2)}, u32[]{:S(2)}) async-start(bf16[32,208,128]{2,1,0:T(8,128)(2,1)} %get-tuple-element.31), calls=%async_computation | async-start | bytes 3407872 | tf_op jit(solution)/shard_map/all_to_all | solution.py:399
  38.2 0.0 copy-done
  38.2 0.0 copy-done.1
  38.3 0.1 slice_bitcast_fusion.2
  38.3 0.0 copy-start.4
  38.3 0.0 copy-start.6
  38.4 0.8 copy-done.4
  39.1 1.1 pad_maximum_fusion.1
  40.2 0.0 copy-done.6
  40.2 3.1 %collective-permute-start.3 = (bf16[2,512,512]{2,1,0:T(8,128)(2,1)}, bf16[2,512,512]{2,1,0:T(8,128)(2,1)}, u32[]{:S(2)}, u32[]{:S(2)}) collective-permute-start(bf16[2,512,512]{2,1,0:T(8,128)(2,1)} %pad_maximum_fusion.1), channel_id=1, source_target_pairs={{0,8},{4,12},{8,16},{12,20},{16,24},{20,28},{24,32},{28,36},{32,40... | collective-permute-start | bytes 3145736 | tf_op jit(solution)/shard_map/ppermute | solution.py:361
  43.3 7.8 %delta_rows.1 = (f32[512,1536]{1,0:T(8,128)}, bf16[512,1536]{1,0:T(8,128)(2,1)}) custom-call(bf16[512,1536]{1,0:T(8,128)(2,1)} %q_ref.4, bf16[512,1536]{1,0:T(8,128)(2,1)} %k_ref.3, bf16[12,4,128,256]{3,2,1,0:T(8,128)(2,1)} %get-tuple-element.27.uw_ref, f32[12,8,8,128]{3,2,1,0:T(8,128)} %get-tuple-element.28.l_ref), custom_call_target="tpu_custom_call" | custom-call | flops 8000000000 | tf_op jit(solution)/shard_map/delta_rows/pallas_call | solution.py:402
  51.1 8.7 %collective-permute-done.1.kv2_ref = bf16[2,512,768]{2,1,0:T(8,128)(2,1)} collective-permute-done((bf16[2,512,768]{2,1,0:T(8,128)(2,1)}, bf16[2,512,768]{2,1,0:T(8,128)(2,1)}, u32[]{:S(2)}, u32[]{:S(2)}) %collective-permute-start.1) | collective-permute-done | bytes 1572896 | tf_op jit(solution)/shard_map/ppermute | solution.py:361
  59.7 2.8 %broadcast_select_fusion = bf16[2,512,768]{2,1,0:T(8,128)(2,1)} fusion(bf16[2,512,768]{2,1,0:T(8,128)(2,1)} %collective-permute-done.1.kv2_ref, pred[]{:T(512)S(6)} %eq.5, bf16[1,512,768]{2,1,0:T(8,128)(2,1)} %copy-done.2, bf16[1,512,768]{2,1,0:T(8,128)(2,1)} %copy-done.3), kind=kLoop, calls=%fused_computation.1 | loop fusion | flops 1572864 | bytes 4718593 | tf_op jit(solution)/shard_map/jit(_where)/select_n | solution.py:415
  62.5 0.3 collective-permute-start.2
  62.8 0.0 all-to-all-done.in_ref
  62.8 6.4 %delta_chain.1 = bf16[32,64,128]{2,1,0:T(8,128)(2,1)} custom-call(bf16[32,208,128]{2,1,0:T(8,128)(2,1)} %all-to-all-done.in_ref), custom_call_target="tpu_custom_call" | custom-call | flops 5000000000 | tf_op jit(solution)/shard_map/delta_chain/pallas_call | solution.py:420
  69.2 13.0 %collective-permute-done.3.kv2_ref = bf16[2,512,512]{2,1,0:T(8,128)(2,1)} collective-permute-done((bf16[2,512,512]{2,1,0:T(8,128)(2,1)}, bf16[2,512,512]{2,1,0:T(8,128)(2,1)}, u32[]{:S(2)}, u32[]{:S(2)}) %collective-permute-start.3) | collective-permute-done | bytes 1048608 | tf_op jit(solution)/shard_map/ppermute | solution.py:361
  82.2 0.0 copy-done.5
  82.2 2.2 %broadcast_select_fusion.1 = bf16[2,512,512]{2,1,0:T(8,128)(2,1)} fusion(bf16[2,512,512]{2,1,0:T(8,128)(2,1)} %collective-permute-done.3.kv2_ref, pred[]{:T(512)S(6)} %eq.5, bf16[1,512,512]{2,1,0:T(8,128)(2,1)S(1)} %copy-done.5, bf16[1,512,512]{2,1,0:T(8,128)(2,1)} %copy-done.6), kind=kLoop, calls=%fused_computation.3 | loop fusion | flops 1048576 | bytes 3145729 | tf_op jit(solution)/shard_map/jit(_where)/select_n | solution.py:415
  84.4 1.6 %collective-permute-start.5 = (bf16[2,512,512]{2,1,0:T(8,128)(2,1)}, bf16[2,512,512]{2,1,0:T(8,128)(2,1)}, u32[]{:S(2)}, u32[]{:S(2)}) collective-permute-start(bf16[2,512,512]{2,1,0:T(8,128)(2,1)} %broadcast_select_fusion.1), channel_id=1, source_target_pairs={{0,4},{4,0},{8,12},{12,8},{16,20},{20,16},{24,28},{28,24},{32,36},... | collective-permute-start | bytes 3145736 | tf_op jit(solution)/shard_map/ppermute | solution.py:361
  86.0 0.0 copy-start.7
  86.0 0.7 copy-done.7
  86.7 0.1 pad_maximum_fusion.2
  86.8 3.5 %collective-permute-start = (bf16[2,512,256]{2,1,0:T(8,128)(2,1)S(1)}, bf16[2,512,256]{2,1,0:T(8,128)(2,1)S(1)}, u32[]{:S(2)}, u32[]{:S(2)}) collective-permute-start(bf16[2,512,256]{2,1,0:T(8,128)(2,1)S(1)} %pad_maximum_fusion.2), channel_id=1, source_target_pairs={{0,8},{4,12},{8,16},{12,20},{16,24},{20,28},{24,32},{28,36},{32,40... | collective-permute-start | bytes 1572872 | tf_op jit(solution)/shard_map/ppermute | solution.py:361
  90.3 9.0 %all-to-all-start.1 = ((bf16[32,64,128]{2,1,0:T(8,128)(2,1)}), bf16[32,64,128]{2,1,0:T(8,128)(2,1)S(1)}, u32[]{:S(2)}, u32[]{:S(2)}) async-start(bf16[32,64,128]{2,1,0:T(8,128)(2,1)} %delta_chain.1), calls=%async_computation.1 | async-start | bytes 1048576 | tf_op jit(solution)/shard_map/all_to_all | solution.py:450
  99.4 0.0 copy-done.14
  99.4 0.6 reshape.18.refs_4_
  100.0 0.0 copy-done.15
  100.0 0.6 reshape.19.refs_5_
  100.6 0.0 collective-permute-done.2.kv1_ref
  100.6 0.6 broadcast_in_dim.3.prev_ref
  101.2 8.5 %window_attention_0.1 = (f32[512,768]{1,0:T(8,128)}, f32[8,128]{1,0:T(8,128)}) custom-call(s32[1]{0:T(128)} %bitcast.idx_ref, bf16[512,1536]{1,0:T(8,128)(2,1)} %q_ref.7, bf16[512,1536]{1,0:T(8,128)(2,1)} %k0_ref.5, bf16[512,1536]{1,0:T(8,128)(2,1)} %v0_ref.5, bf16[2,512,768]{2,1,0:T(8,128)(2,1)} %collective-permute-done.2.kv1_ref, ...), custom_call_target="tpu_custom_call" | custom-call | flops 1000000000 | tf_op jit(solution)/shard_map/window_attention_0/pallas_call | solution.py:436
  109.7 0.0 collective-permute-done.kv2_ref
  109.7 0.0 copy-done.8
  109.7 0.1 broadcast_select_fusion.2
  109.8 1.5 collective-permute-start.4
  111.3 15.5 %collective-permute-done.5.kv1_ref = bf16[2,512,512]{2,1,0:T(8,128)(2,1)} collective-permute-done((bf16[2,512,512]{2,1,0:T(8,128)(2,1)}, bf16[2,512,512]{2,1,0:T(8,128)(2,1)}, u32[]{:S(2)}, u32[]{:S(2)}) %collective-permute-start.5) | collective-permute-done | bytes 1048608 | tf_op jit(solution)/shard_map/ppermute | solution.py:361
  126.9 6.7 %window_attention_1.1 = (f32[512,512]{1,0:T(8,128)}, f32[8,128]{1,0:T(8,128)}) custom-call(s32[1]{0:T(128)} %bitcast.idx_ref, bf16[512,1536]{1,0:T(8,128)(2,1)} %q_ref.7, bf16[512,1536]{1,0:T(8,128)(2,1)} %k0_ref.5, bf16[512,1536]{1,0:T(8,128)(2,1)} %v0_ref.5, bf16[2,512,512]{2,1,0:T(8,128)(2,1)} %collective-permute-done.5.kv1_ref, ...), custom_call_target="tpu_custom_call" | custom-call | flops 1000000000 | tf_op jit(solution)/shard_map/window_attention_1/pallas_call | solution.py:436
  133.5 0.0 copy-done.9
  133.5 0.0 all-to-all-done.1.t_ref
  133.5 0.0 copy-start.10
  133.5 0.8 copy-done.10
  134.3 7.4 %delta_apply.1 = (f32[512,1536]{1,0:T(8,128)}, f32[8,128]{1,0:T(8,128)}) custom-call(f32[512,1536]{1,0:T(8,128)} %get-tuple-element.36.o_ref, bf16[512,1536]{1,0:T(8,128)(2,1)} %get-tuple-element.37.y_ref, bf16[12,3,128,256]{3,2,1,0:T(8,128)(2,1)} %get-tuple-element.38.m_ref, bf16[32,64,128]{2,1,0:T(8,128)(2,1)} %copy-done.10, ...), custom_call_target="tpu_custom_call" | custom-call | flops 5000000000 | tf_op jit(solution)/shard_map/delta_apply/pallas_call | solution.py:460
  141.7 0.0 collective-permute-done.4.kv1_ref
  141.7 0.8 copy-done.11
  142.5 4.2 %window_attention_2.1 = (f32[512,256]{1,0:T(8,128)}, f32[8,128]{1,0:T(8,128)}) custom-call(s32[1]{0:T(128)} %bitcast.idx_ref, bf16[512,1536]{1,0:T(8,128)(2,1)} %q_ref.7, bf16[512,1536]{1,0:T(8,128)(2,1)} %k0_ref.5, bf16[512,1536]{1,0:T(8,128)(2,1)} %v0_ref.5, bf16[2,512,256]{2,1,0:T(8,128)(2,1)} %copy-done.11, bf16[2,512,256]{2,1,0:T(8,128)(2,1)} %copy-done.9, ...), custom_call_target="tpu_custom_call" | custom-call | flops 1000000000 | tf_op jit(solution)/shard_map/window_attention_2/pallas_call | solution.py:436
  146.7 7.8 %psum.7.sq_ref = f32[8,128]{1,0:T(8,128)} all-reduce(f32[8,128]{1,0:T(8,128)} %get-tuple-element.44), channel_id=1, replica_groups=mesh['ctx'=32,'head'=4] {'head'}, use_global_device_ids=true, to_apply=%region_0.1 | all-reduce | flops 1024 | bytes 8192 | tf_op jit(solution)/shard_map/psum | solution.py:474
  154.5 4.9 %join.1 = bf16[512,1536]{1,0:T(8,128)(2,1)} custom-call(f32[8,128]{1,0:T(8,128)} %psum.7.sq_ref, f32[512,768]{1,0:T(8,128)} %get-tuple-element.45.refs_0_, f32[512,512]{1,0:T(8,128)} %get-tuple-element.46.refs_1_, f32[512,256]{1,0:T(8,128)} %get-tuple-element.47.refs_2_, f32[512,1536]{1,0:T(8,128)} %get-tuple-element.48.refs_3_, f32[1,1536]{1,0:T(1,128)} %reshape.18.refs_4_, ...), custom_call_target="tpu_custom_call" | custom-call | tf_op jit(solution)/shard_map/join/pallas_call | solution.py:478
  (7 shorter events, 0.0 us)
Async XLA Ops:
  1.5 1.5 copy-start.2
  1.5 1.7 %copy-start.3 = (bf16[1,512,768]{2,1,0:T(8,128)(2,1)}, bf16[1,512,768]{2,1,0:T(8,128)(2,1)S(1)}, u32[]{:S(2)}) copy-start(bf16[1,512,768]{2,1,0:T(8,128)(2,1)S(1)} %get-tuple-element.52) | copy-start | bytes 2359300
  1.5 5.2 %copy-start.12 = (f32[512,12]{0,1:T(8,128)S(1)}, f32[512,12]{0,1:T(8,128)}, u32[]{:S(2)}) copy-start(f32[512,12]{0,1:T(8,128)} %param.16) | copy-start | bytes 73732
  1.5 5.8 %copy-start.13 = (f32[512,12]{0,1:T(8,128)S(1)}, f32[512,12]{0,1:T(8,128)}, u32[]{:S(2)}) copy-start(f32[512,12]{0,1:T(8,128)} %param.17) | copy-start | bytes 73732
  3.1 56.6 %collective-permute-start.1 = (bf16[2,512,768]{2,1,0:T(8,128)(2,1)}, bf16[2,512,768]{2,1,0:T(8,128)(2,1)}, u32[]{:S(2)}, u32[]{:S(2)}) collective-permute-start(bf16[2,512,768]{2,1,0:T(8,128)(2,1)} %pad_maximum_fusion), channel_id=1, source_target_pairs={{0,8},{4,12},{8,16},{12,20},{16,24},{20,28},{24,32},{28,36},{32,40... | collective-permute-start | bytes 4718600 | tf_op jit(solution)/shard_map/ppermute | solution.py:361
  29.8 8.4 %copy-start = (bf16[512,1536]{1,0:T(8,128)(2,1)S(1)}, bf16[512,1536]{1,0:T(8,128)(2,1)}, u32[]{:S(2)}) copy-start(bf16[512,1536]{1,0:T(8,128)(2,1)} %k0_ref.5) | copy-start | bytes 4718596
  29.8 8.5 %copy-start.1 = (bf16[512,1536]{1,0:T(8,128)(2,1)S(1)}, bf16[512,1536]{1,0:T(8,128)(2,1)}, u32[]{:S(2)}) copy-start(bf16[512,1536]{1,0:T(8,128)(2,1)} %v0_ref.5) | copy-start | bytes 4718596
  29.8 33.0 %all-to-all-start = ((bf16[32,208,128]{2,1,0:T(8,128)(2,1)}), bf16[32,208,128]{2,1,0:T(8,128)(2,1)}, u32[]{:S(2)}, u32[]{:S(2)}) async-start(bf16[32,208,128]{2,1,0:T(8,128)(2,1)} %get-tuple-element.31), calls=%async_computation | async-start | bytes 3407872 | tf_op jit(solution)/shard_map/all_to_all | solution.py:399
  38.3 0.8 copy-start.4
  38.3 1.9 %copy-start.6 = (bf16[1,512,512]{2,1,0:T(8,128)(2,1)}, bf16[1,512,512]{2,1,0:T(8,128)(2,1)S(1)}, u32[]{:S(2)}) copy-start(bf16[1,512,512]{2,1,0:T(8,128)(2,1)S(1)} %get-tuple-element.54) | copy-start | bytes 1572868
  40.2 42.0 %collective-permute-start.3 = (bf16[2,512,512]{2,1,0:T(8,128)(2,1)}, bf16[2,512,512]{2,1,0:T(8,128)(2,1)}, u32[]{:S(2)}, u32[]{:S(2)}) collective-permute-start(bf16[2,512,512]{2,1,0:T(8,128)(2,1)} %pad_maximum_fusion.1), channel_id=1, source_target_pairs={{0,8},{4,12},{8,16},{12,20},{16,24},{20,28},{24,32},{28,36},{32,40... | collective-permute-start | bytes 3145736 | tf_op jit(solution)/shard_map/ppermute | solution.py:361
  62.5 38.0 %collective-permute-start.2 = (bf16[2,512,768]{2,1,0:T(8,128)(2,1)}, bf16[2,512,768]{2,1,0:T(8,128)(2,1)}, u32[]{:S(2)}, u32[]{:S(2)}) collective-permute-start(bf16[2,512,768]{2,1,0:T(8,128)(2,1)} %broadcast_select_fusion), channel_id=1, source_target_pairs={{0,4},{4,0},{8,12},{12,8},{16,20},{20,16},{24,28},{28,24},{32,36},... | collective-permute-start | bytes 4718600 | tf_op jit(solution)/shard_map/ppermute | solution.py:361
  62.8 19.4 %copy-start.5 = (bf16[1,512,512]{2,1,0:T(8,128)(2,1)S(1)}, bf16[1,512,512]{2,1,0:T(8,128)(2,1)}, u32[]{:S(2)}) copy-start(bf16[1,512,512]{2,1,0:T(8,128)(2,1)} %copy-done.4) | copy-start | bytes 1572868
  84.4 15.0 %copy-start.14 = (f32[1536]{0:T(1024)S(1)}, f32[1536]{0:T(1024)}, u32[]{:S(2)}) copy-start(f32[1536]{0:T(1024)} %param.18) | copy-start | bytes 18436
  84.4 15.6 %copy-start.15 = (f32[1536]{0:T(1024)S(1)}, f32[1536]{0:T(1024)}, u32[]{:S(2)}) copy-start(f32[1536]{0:T(1024)} %param.19) | copy-start | bytes 18436
  84.4 42.5 %collective-permute-start.5 = (bf16[2,512,512]{2,1,0:T(8,128)(2,1)}, bf16[2,512,512]{2,1,0:T(8,128)(2,1)}, u32[]{:S(2)}, u32[]{:S(2)}) collective-permute-start(bf16[2,512,512]{2,1,0:T(8,128)(2,1)} %broadcast_select_fusion.1), channel_id=1, source_target_pairs={{0,4},{4,0},{8,12},{12,8},{16,20},{20,16},{24,28},{28,24},{32,36},... | collective-permute-start | bytes 3145736 | tf_op jit(solution)/shard_map/ppermute | solution.py:361
  86.0 0.7 copy-start.7
  86.8 22.9 %collective-permute-start = (bf16[2,512,256]{2,1,0:T(8,128)(2,1)S(1)}, bf16[2,512,256]{2,1,0:T(8,128)(2,1)S(1)}, u32[]{:S(2)}, u32[]{:S(2)}) collective-permute-start(bf16[2,512,256]{2,1,0:T(8,128)(2,1)S(1)} %pad_maximum_fusion.2), channel_id=1, source_target_pairs={{0,8},{4,12},{8,16},{12,20},{16,24},{20,28},{24,32},{28,36},{32,40... | collective-permute-start | bytes 1572872 | tf_op jit(solution)/shard_map/ppermute | solution.py:361
  90.3 43.2 %all-to-all-start.1 = ((bf16[32,64,128]{2,1,0:T(8,128)(2,1)}), bf16[32,64,128]{2,1,0:T(8,128)(2,1)S(1)}, u32[]{:S(2)}, u32[]{:S(2)}) async-start(bf16[32,64,128]{2,1,0:T(8,128)(2,1)} %delta_chain.1), calls=%async_computation.1 | async-start | bytes 1048576 | tf_op jit(solution)/shard_map/all_to_all | solution.py:450
  101.2 8.5 %copy-start.8 = (bf16[1,512,256]{2,1,0:T(8,128)(2,1)S(1)}, bf16[1,512,256]{2,1,0:T(8,128)(2,1)}, u32[]{:S(2)}) copy-start(bf16[1,512,256]{2,1,0:T(8,128)(2,1)} %copy-done.7) | copy-start | bytes 786436
  109.7 23.8 %copy-start.9 = (bf16[2,512,256]{2,1,0:T(8,128)(2,1)}, bf16[2,512,256]{2,1,0:T(8,128)(2,1)S(1)}, u32[]{:S(2)}) copy-start(bf16[2,512,256]{2,1,0:T(8,128)(2,1)S(1)} %collective-permute-done.kv2_ref) | copy-start | bytes 1572868
  109.8 31.9 %collective-permute-start.4 = (bf16[2,512,256]{2,1,0:T(8,128)(2,1)S(1)}, bf16[2,512,256]{2,1,0:T(8,128)(2,1)S(1)}, u32[]{:S(2)}, u32[]{:S(2)}) collective-permute-start(bf16[2,512,256]{2,1,0:T(8,128)(2,1)S(1)} %broadcast_select_fusion.2), channel_id=1, source_target_pairs={{0,4},{4,0},{8,12},{12,8},{16,20},{20,16},{24,28},{28,24},{32,36},... | collective-permute-start | bytes 1572872 | tf_op jit(solution)/shard_map/ppermute | solution.py:361
  133.5 0.8 copy-start.10
  141.7 0.8 copy-start.11

commit v3 on v2

--- a/solution.py
+++ b/solution.py
@@ -327,8 +327,13 @@
     scales = jnp.transpose(0.5 * lax.rsqrt(sq_ref[...] * (1.0 / WIDTH) + EPS))
     lane = lax.broadcasted_iota(jnp.int32, scales.shape, 1)
     i = pl.program_id(0)
-    attn_scale = jnp.sum(jnp.where(lane == i, scales, 0.0), axis=1, keepdims=True)
-    delta_scale = jnp.sum(jnp.where(lane == i + n, scales, 0.0), axis=1, keepdims=True)
+    per = o_ref.shape[0] // DH
+
+    def column(first):
+        parts = [jnp.sum(jnp.where(lane == first + k, scales, 0.0), axis=1, keepdims=True) for k in range(per)]
+        return cat(parts, 0)
+
+    attn_scale, delta_scale = column(i * per), column(i * per + n)
     at = 0
     for a_ref in a_refs:
         lanes = slice(at, at + a_ref.shape[1])
@@ -473,12 +478,13 @@
     attn.append(out)
     squares = lax.psum(squares, "head")
 
-    cols = pl.BlockSpec((DH, width), lambda i: (i, 0))
+    block = 2 * DH
+    cols = pl.BlockSpec((block, width), lambda i: (i, 0))
     gains = pl.BlockSpec((1, width), lambda i: (0, 0))
     return pl.pallas_call(
         join_kernel,
-        grid=(rows // DH,),
-        in_specs=[whole] + [pl.BlockSpec((DH, size), lambda i: (i, 0)) for _, size in parts] + [cols, gains, gains],
+        grid=(rows // block,),
+        in_specs=[whole] + [pl.BlockSpec((block, size), lambda i: (i, 0)) for _, size in parts] + [cols, gains, gains],
         out_specs=cols,
         out_shape=shaped((rows, width), bf16),
         compiler_params=params(),

time: 160 us -> 160 us (level)
  no operation moved by 1% of the time
where the time goes in v3:
time: 160 us; the launch traced here: 159 us
  Pallas kernels  67 us (42%)
  waiting for transfers between devices  37.2 us (23%)
  starting transfers between devices  31 us (19%)
  local copies, waits for them, and re-layouts  7.92 us (5%)
  blocking collectives  7.83 us (5%)
  other arithmetic  7.56 us (5%)
    ppermute x6, waiting for transfers between devices, send(): return lax.ppermute(x, 'ctx', pairs)  37.2 us
    pallas_call x1, Pallas kernels, on_device(): pl.pallas_call(map_kernel, grid=(heads // hb,), in_specs=[wide(hb), wide(...  21.8 us
    pallas_call x3, Pallas kernels, attend(): pl.pallas_call(functools.partial(attn_kernel, QB=QB), grid=(steps,), in_s...  19.4 us
    ppermute x6, starting transfers between devices, send(): return lax.ppermute(x, 'ctx', pairs)  13.6 us
    all_to_all x1, starting transfers between devices, on_device(): states = lax.all_to_all(chain, 'ctx', 0, 0, tiled=True)  9.04 us
    all_to_all x1, starting transfers between devices, on_device(): got = lax.all_to_all(pay, 'ctx', 0, 0, tiled=True)  8.42 us
    psum x1, blocking collectives, on_device(): squares = lax.psum(squares, 'head')  7.83 us
    pallas_call x1, Pallas kernels, on_device(): pl.pallas_call(out_kernel, grid=(heads // hb,), in_specs=[wide(hb), wide(...  7.76 us
  transfers between devices with their start and end apart: 8, of which 3 were waited for; matrix products, arithmetic and copies ran while one was open for 6% of the time, Pallas kernels for 37%

profile of v3, /device:TPU:84, one launch (start us, length us, event | category | flops | bytes accessed | tf_op | source)
XLA Modules:
  0.0 158.8 jit_solution(1748673610596253809)
XLA Ops:
  0.0 1.5 slice_bitcast_fusion
  1.5 0.0 copy-start.2
  1.5 0.0 copy-start.3
  1.5 0.0 copy-start.12
  1.5 0.0 copy-start.13
  1.5 1.4 pad_maximum_fusion
  2.9 0.0 copy-done.2
  2.9 0.2 copy-done.3
  3.1 3.5 %collective-permute-start.1 = (bf16[2,512,768]{2,1,0:T(8,128)(2,1)}, bf16[2,512,768]{2,1,0:T(8,128)(2,1)}, u32[]{:S(2)}, u32[]{:S(2)}) collective-permute-start(bf16[2,512,768]{2,1,0:T(8,128)(2,1)} %pad_maximum_fusion), channel_id=1, source_target_pairs={{0,8},{4,12},{8,16},{12,20},{16,24},{20,28},{24,32},{28,36},{32,40... | collective-permute-start | bytes 4718600 | tf_op jit(solution)/shard_map/ppermute | solution.py:366
  6.7 0.0 copy-done.12
  6.7 0.6 reshape.16.g_ref
  7.3 0.0 copy-done.13
  7.3 0.6 reshape.17.b_ref
  7.9 21.8 %delta_maps.1 = (bf16[12,4,128,256]{3,2,1,0:T(8,128)(2,1)}, bf16[12,3,128,256]{3,2,1,0:T(8,128)(2,1)}, f32[12,8,8,128]{3,2,1,0:T(8,128)}, bf16[32,208,128]{2,1,0:T(8,128)(2,1)}) custom-call(bf16[512,1536]{1,0:T(8,128)(2,1)} %k_ref.3, bf16[512,1536]{1,0:T(8,128)(2,1)} %v_ref.1, f32[12,1,512]{2,1,0:T(1,128)} %reshape.16.g_ref, f32[12,1,512]{2,1,0:T(1,128)} %reshape.17.b_ref), custom_call_target="tpu_custom_call" | custom-call | flops 2000000000 | tf_op jit(solution)/shard_map/delta_maps/pallas_call | solution.py:388
  29.8 0.0 copy-start
  29.8 0.0 copy-start.1
  29.8 8.4 %all-to-all-start = ((bf16[32,208,128]{2,1,0:T(8,128)(2,1)}), bf16[32,208,128]{2,1,0:T(8,128)(2,1)}, u32[]{:S(2)}, u32[]{:S(2)}) async-start(bf16[32,208,128]{2,1,0:T(8,128)(2,1)} %get-tuple-element.31), calls=%async_computation | async-start | bytes 3407872 | tf_op jit(solution)/shard_map/all_to_all | solution.py:404
  38.2 0.0 copy-done
  38.2 0.0 copy-done.1
  38.3 0.1 slice_bitcast_fusion.2
  38.3 0.0 copy-start.4
  38.3 0.0 copy-start.6
  38.4 0.8 copy-done.4
  39.1 1.1 pad_maximum_fusion.1
  40.2 0.0 copy-done.6
  40.2 3.1 %collective-permute-start.3 = (bf16[2,512,512]{2,1,0:T(8,128)(2,1)}, bf16[2,512,512]{2,1,0:T(8,128)(2,1)}, u32[]{:S(2)}, u32[]{:S(2)}) collective-permute-start(bf16[2,512,512]{2,1,0:T(8,128)(2,1)} %pad_maximum_fusion.1), channel_id=1, source_target_pairs={{0,8},{4,12},{8,16},{12,20},{16,24},{20,28},{24,32},{28,36},{32,40... | collective-permute-start | bytes 3145736 | tf_op jit(solution)/shard_map/ppermute | solution.py:366
  43.3 7.8 %delta_rows.1 = (f32[512,1536]{1,0:T(8,128)}, bf16[512,1536]{1,0:T(8,128)(2,1)}) custom-call(bf16[512,1536]{1,0:T(8,128)(2,1)} %q_ref.4, bf16[512,1536]{1,0:T(8,128)(2,1)} %k_ref.3, bf16[12,4,128,256]{3,2,1,0:T(8,128)(2,1)} %get-tuple-element.27.uw_ref, f32[12,8,8,128]{3,2,1,0:T(8,128)} %get-tuple-element.28.l_ref), custom_call_target="tpu_custom_call" | custom-call | flops 8000000000 | tf_op jit(solution)/shard_map/delta_rows/pallas_call | solution.py:407
  51.1 8.7 %collective-permute-done.1.kv2_ref = bf16[2,512,768]{2,1,0:T(8,128)(2,1)} collective-permute-done((bf16[2,512,768]{2,1,0:T(8,128)(2,1)}, bf16[2,512,768]{2,1,0:T(8,128)(2,1)}, u32[]{:S(2)}, u32[]{:S(2)}) %collective-permute-start.1) | collective-permute-done | bytes 1572896 | tf_op jit(solution)/shard_map/ppermute | solution.py:366
  59.7 2.8 %broadcast_select_fusion = bf16[2,512,768]{2,1,0:T(8,128)(2,1)} fusion(bf16[2,512,768]{2,1,0:T(8,128)(2,1)} %collective-permute-done.1.kv2_ref, pred[]{:T(512)S(6)} %eq.5, bf16[1,512,768]{2,1,0:T(8,128)(2,1)} %copy-done.2, bf16[1,512,768]{2,1,0:T(8,128)(2,1)} %copy-done.3), kind=kLoop, calls=%fused_computation.1 | loop fusion | flops 1572864 | bytes 4718593 | tf_op jit(solution)/shard_map/jit(_where)/select_n | solution.py:420
  62.5 0.3 collective-permute-start.2
  62.8 0.0 all-to-all-done.in_ref
  62.8 6.4 %delta_chain.1 = bf16[32,64,128]{2,1,0:T(8,128)(2,1)} custom-call(bf16[32,208,128]{2,1,0:T(8,128)(2,1)} %all-to-all-done.in_ref), custom_call_target="tpu_custom_call" | custom-call | flops 5000000000 | tf_op jit(solution)/shard_map/delta_chain/pallas_call | solution.py:425
  69.2 13.0 %collective-permute-done.3.kv2_ref = bf16[2,512,512]{2,1,0:T(8,128)(2,1)} collective-permute-done((bf16[2,512,512]{2,1,0:T(8,128)(2,1)}, bf16[2,512,512]{2,1,0:T(8,128)(2,1)}, u32[]{:S(2)}, u32[]{:S(2)}) %collective-permute-start.3) | collective-permute-done | bytes 1048608 | tf_op jit(solution)/shard_map/ppermute | solution.py:366
  82.2 0.0 copy-done.5
  82.2 2.2 %broadcast_select_fusion.1 = bf16[2,512,512]{2,1,0:T(8,128)(2,1)} fusion(bf16[2,512,512]{2,1,0:T(8,128)(2,1)} %collective-permute-done.3.kv2_ref, pred[]{:T(512)S(6)} %eq.5, bf16[1,512,512]{2,1,0:T(8,128)(2,1)S(1)} %copy-done.5, bf16[1,512,512]{2,1,0:T(8,128)(2,1)} %copy-done.6), kind=kLoop, calls=%fused_computation.3 | loop fusion | flops 1048576 | bytes 3145729 | tf_op jit(solution)/shard_map/jit(_where)/select_n | solution.py:420
  84.4 1.6 %collective-permute-start.5 = (bf16[2,512,512]{2,1,0:T(8,128)(2,1)}, bf16[2,512,512]{2,1,0:T(8,128)(2,1)}, u32[]{:S(2)}, u32[]{:S(2)}) collective-permute-start(bf16[2,512,512]{2,1,0:T(8,128)(2,1)} %broadcast_select_fusion.1), channel_id=1, source_target_pairs={{0,4},{4,0},{8,12},{12,8},{16,20},{20,16},{24,28},{28,24},{32,36},... | collective-permute-start | bytes 3145736 | tf_op jit(solution)/shard_map/ppermute | solution.py:366
  86.0 0.0 copy-start.7
  86.0 0.7 copy-done.7
  86.7 0.1 pad_maximum_fusion.2
  86.8 3.5 %collective-permute-start = (bf16[2,512,256]{2,1,0:T(8,128)(2,1)S(1)}, bf16[2,512,256]{2,1,0:T(8,128)(2,1)S(1)}, u32[]{:S(2)}, u32[]{:S(2)}) collective-permute-start(bf16[2,512,256]{2,1,0:T(8,128)(2,1)S(1)} %pad_maximum_fusion.2), channel_id=1, source_target_pairs={{0,8},{4,12},{8,16},{12,20},{16,24},{20,28},{24,32},{28,36},{32,40... | collective-permute-start | bytes 1572872 | tf_op jit(solution)/shard_map/ppermute | solution.py:366
  90.3 9.0 %all-to-all-start.1 = ((bf16[32,64,128]{2,1,0:T(8,128)(2,1)}), bf16[32,64,128]{2,1,0:T(8,128)(2,1)S(1)}, u32[]{:S(2)}, u32[]{:S(2)}) async-start(bf16[32,64,128]{2,1,0:T(8,128)(2,1)} %delta_chain.1), calls=%async_computation.1 | async-start | bytes 1048576 | tf_op jit(solution)/shard_map/all_to_all | solution.py:455
  99.4 0.0 copy-done.14
  99.4 0.6 reshape.18.refs_4_
  100.0 0.0 copy-done.15
  100.0 0.6 reshape.19.refs_5_
  100.6 0.0 collective-permute-done.2.kv1_ref
  100.6 0.6 broadcast_in_dim.3.prev_ref
  101.2 8.5 %window_attention_0.1 = (f32[512,768]{1,0:T(8,128)}, f32[8,128]{1,0:T(8,128)}) custom-call(s32[1]{0:T(128)} %bitcast.idx_ref, bf16[512,1536]{1,0:T(8,128)(2,1)} %q_ref.7, bf16[512,1536]{1,0:T(8,128)(2,1)} %k0_ref.5, bf16[512,1536]{1,0:T(8,128)(2,1)} %v0_ref.5, bf16[2,512,768]{2,1,0:T(8,128)(2,1)} %collective-permute-done.2.kv1_ref, ...), custom_call_target="tpu_custom_call" | custom-call | flops 1000000000 | tf_op jit(solution)/shard_map/window_attention_0/pallas_call | solution.py:441
  109.7 0.0 collective-permute-done.kv2_ref
  109.7 0.0 copy-done.8
  109.7 0.1 broadcast_select_fusion.2
  109.8 1.5 collective-permute-start.4
  111.3 15.5 %collective-permute-done.5.kv1_ref = bf16[2,512,512]{2,1,0:T(8,128)(2,1)} collective-permute-done((bf16[2,512,512]{2,1,0:T(8,128)(2,1)}, bf16[2,512,512]{2,1,0:T(8,128)(2,1)}, u32[]{:S(2)}, u32[]{:S(2)}) %collective-permute-start.5) | collective-permute-done | bytes 1048608 | tf_op jit(solution)/shard_map/ppermute | solution.py:366
  126.9 6.7 %window_attention_1.1 = (f32[512,512]{1,0:T(8,128)}, f32[8,128]{1,0:T(8,128)}) custom-call(s32[1]{0:T(128)} %bitcast.idx_ref, bf16[512,1536]{1,0:T(8,128)(2,1)} %q_ref.7, bf16[512,1536]{1,0:T(8,128)(2,1)} %k0_ref.5, bf16[512,1536]{1,0:T(8,128)(2,1)} %v0_ref.5, bf16[2,512,512]{2,1,0:T(8,128)(2,1)} %collective-permute-done.5.kv1_ref, ...), custom_call_target="tpu_custom_call" | custom-call | flops 1000000000 | tf_op jit(solution)/shard_map/window_attention_1/pallas_call | solution.py:441
  133.5 0.0 copy-done.9
  133.5 0.0 all-to-all-done.1.t_ref
  133.5 0.0 copy-start.10
  133.5 0.8 copy-done.10
  134.3 7.4 %delta_apply.1 = (f32[512,1536]{1,0:T(8,128)}, f32[8,128]{1,0:T(8,128)}) custom-call(f32[512,1536]{1,0:T(8,128)} %get-tuple-element.36.o_ref, bf16[512,1536]{1,0:T(8,128)(2,1)} %get-tuple-element.37.y_ref, bf16[12,3,128,256]{3,2,1,0:T(8,128)(2,1)} %get-tuple-element.38.m_ref, bf16[32,64,128]{2,1,0:T(8,128)(2,1)} %copy-done.10, ...), custom_call_target="tpu_custom_call" | custom-call | flops 5000000000 | tf_op jit(solution)/shard_map/delta_apply/pallas_call | solution.py:465
  141.7 0.0 collective-permute-done.4.kv1_ref
  141.7 0.8 copy-done.11
  142.5 4.2 %window_attention_2.1 = (f32[512,256]{1,0:T(8,128)}, f32[8,128]{1,0:T(8,128)}) custom-call(s32[1]{0:T(128)} %bitcast.idx_ref, bf16[512,1536]{1,0:T(8,128)(2,1)} %q_ref.7, bf16[512,1536]{1,0:T(8,128)(2,1)} %k0_ref.5, bf16[512,1536]{1,0:T(8,128)(2,1)} %v0_ref.5, bf16[2,512,256]{2,1,0:T(8,128)(2,1)} %copy-done.11, bf16[2,512,256]{2,1,0:T(8,128)(2,1)} %copy-done.9, ...), custom_call_target="tpu_custom_call" | custom-call | flops 1000000000 | tf_op jit(solution)/shard_map/window_attention_2/pallas_call | solution.py:441
  146.7 7.8 %psum.7.sq_ref = f32[8,128]{1,0:T(8,128)} all-reduce(f32[8,128]{1,0:T(8,128)} %get-tuple-element.44), channel_id=1, replica_groups=mesh['ctx'=32,'head'=4] {'head'}, use_global_device_ids=true, to_apply=%region_0.1 | all-reduce | flops 1024 | bytes 8192 | tf_op jit(solution)/shard_map/psum | solution.py:479
  154.5 4.3 %join.1 = bf16[512,1536]{1,0:T(8,128)(2,1)} custom-call(f32[8,128]{1,0:T(8,128)} %psum.7.sq_ref, f32[512,768]{1,0:T(8,128)} %get-tuple-element.45.refs_0_, f32[512,512]{1,0:T(8,128)} %get-tuple-element.46.refs_1_, f32[512,256]{1,0:T(8,128)} %get-tuple-element.47.refs_2_, f32[512,1536]{1,0:T(8,128)} %get-tuple-element.48.refs_3_, f32[1,1536]{1,0:T(1,128)} %reshape.18.refs_4_, ...), custom_call_target="tpu_custom_call" | custom-call | tf_op jit(solution)/shard_map/join/pallas_call | solution.py:484
  (7 shorter events, 0.0 us)
Async XLA Ops:
  1.5 1.5 copy-start.2
  1.5 1.7 %copy-start.3 = (bf16[1,512,768]{2,1,0:T(8,128)(2,1)}, bf16[1,512,768]{2,1,0:T(8,128)(2,1)S(1)}, u32[]{:S(2)}) copy-start(bf16[1,512,768]{2,1,0:T(8,128)(2,1)S(1)} %get-tuple-element.52) | copy-start | bytes 2359300
  1.5 5.2 %copy-start.12 = (f32[512,12]{0,1:T(8,128)S(1)}, f32[512,12]{0,1:T(8,128)}, u32[]{:S(2)}) copy-start(f32[512,12]{0,1:T(8,128)} %param.16) | copy-start | bytes 73732
  1.5 5.8 %copy-start.13 = (f32[512,12]{0,1:T(8,128)S(1)}, f32[512,12]{0,1:T(8,128)}, u32[]{:S(2)}) copy-start(f32[512,12]{0,1:T(8,128)} %param.17) | copy-start | bytes 73732
  3.1 56.6 %collective-permute-start.1 = (bf16[2,512,768]{2,1,0:T(8,128)(2,1)}, bf16[2,512,768]{2,1,0:T(8,128)(2,1)}, u32[]{:S(2)}, u32[]{:S(2)}) collective-permute-start(bf16[2,512,768]{2,1,0:T(8,128)(2,1)} %pad_maximum_fusion), channel_id=1, source_target_pairs={{0,8},{4,12},{8,16},{12,20},{16,24},{20,28},{24,32},{28,36},{32,40... | collective-permute-start | bytes 4718600 | tf_op jit(solution)/shard_map/ppermute | solution.py:366
  29.8 8.4 %copy-start = (bf16[512,1536]{1,0:T(8,128)(2,1)S(1)}, bf16[512,1536]{1,0:T(8,128)(2,1)}, u32[]{:S(2)}) copy-start(bf16[512,1536]{1,0:T(8,128)(2,1)} %k0_ref.5) | copy-start | bytes 4718596
  29.8 8.5 %copy-start.1 = (bf16[512,1536]{1,0:T(8,128)(2,1)S(1)}, bf16[512,1536]{1,0:T(8,128)(2,1)}, u32[]{:S(2)}) copy-start(bf16[512,1536]{1,0:T(8,128)(2,1)} %v0_ref.5) | copy-start | bytes 4718596
  29.8 33.0 %all-to-all-start = ((bf16[32,208,128]{2,1,0:T(8,128)(2,1)}), bf16[32,208,128]{2,1,0:T(8,128)(2,1)}, u32[]{:S(2)}, u32[]{:S(2)}) async-start(bf16[32,208,128]{2,1,0:T(8,128)(2,1)} %get-tuple-element.31), calls=%async_computation | async-start | bytes 3407872 | tf_op jit(solution)/shard_map/all_to_all | solution.py:404
  38.3 0.8 copy-start.4
  38.3 1.9 %copy-start.6 = (bf16[1,512,512]{2,1,0:T(8,128)(2,1)}, bf16[1,512,512]{2,1,0:T(8,128)(2,1)S(1)}, u32[]{:S(2)}) copy-start(bf16[1,512,512]{2,1,0:T(8,128)(2,1)S(1)} %get-tuple-element.54) | copy-start | bytes 1572868
  40.2 42.0 %collective-permute-start.3 = (bf16[2,512,512]{2,1,0:T(8,128)(2,1)}, bf16[2,512,512]{2,1,0:T(8,128)(2,1)}, u32[]{:S(2)}, u32[]{:S(2)}) collective-permute-start(bf16[2,512,512]{2,1,0:T(8,128)(2,1)} %pad_maximum_fusion.1), channel_id=1, source_target_pairs={{0,8},{4,12},{8,16},{12,20},{16,24},{20,28},{24,32},{28,36},{32,40... | collective-permute-start | bytes 3145736 | tf_op jit(solution)/shard_map/ppermute | solution.py:366
  62.5 38.0 %collective-permute-start.2 = (bf16[2,512,768]{2,1,0:T(8,128)(2,1)}, bf16[2,512,768]{2,1,0:T(8,128)(2,1)}, u32[]{:S(2)}, u32[]{:S(2)}) collective-permute-start(bf16[2,512,768]{2,1,0:T(8,128)(2,1)} %broadcast_select_fusion), channel_id=1, source_target_pairs={{0,4},{4,0},{8,12},{12,8},{16,20},{20,16},{24,28},{28,24},{32,36},... | collective-permute-start | bytes 4718600 | tf_op jit(solution)/shard_map/ppermute | solution.py:366
  62.8 19.4 %copy-start.5 = (bf16[1,512,512]{2,1,0:T(8,128)(2,1)S(1)}, bf16[1,512,512]{2,1,0:T(8,128)(2,1)}, u32[]{:S(2)}) copy-start(bf16[1,512,512]{2,1,0:T(8,128)(2,1)} %copy-done.4) | copy-start | bytes 1572868
  84.4 15.0 %copy-start.14 = (f32[1536]{0:T(1024)S(1)}, f32[1536]{0:T(1024)}, u32[]{:S(2)}) copy-start(f32[1536]{0:T(1024)} %param.18) | copy-start | bytes 18436
  84.4 15.6 %copy-start.15 = (f32[1536]{0:T(1024)S(1)}, f32[1536]{0:T(1024)}, u32[]{:S(2)}) copy-start(f32[1536]{0:T(1024)} %param.19) | copy-start | bytes 18436
  84.4 42.5 %collective-permute-start.5 = (bf16[2,512,512]{2,1,0:T(8,128)(2,1)}, bf16[2,512,512]{2,1,0:T(8,128)(2,1)}, u32[]{:S(2)}, u32[]{:S(2)}) collective-permute-start(bf16[2,512,512]{2,1,0:T(8,128)(2,1)} %broadcast_select_fusion.1), channel_id=1, source_target_pairs={{0,4},{4,0},{8,12},{12,8},{16,20},{20,16},{24,28},{28,24},{32,36},... | collective-permute-start | bytes 3145736 | tf_op jit(solution)/shard_map/ppermute | solution.py:366
  86.0 0.7 copy-start.7
  86.8 22.9 %collective-permute-start = (bf16[2,512,256]{2,1,0:T(8,128)(2,1)S(1)}, bf16[2,512,256]{2,1,0:T(8,128)(2,1)S(1)}, u32[]{:S(2)}, u32[]{:S(2)}) collective-permute-start(bf16[2,512,256]{2,1,0:T(8,128)(2,1)S(1)} %pad_maximum_fusion.2), channel_id=1, source_target_pairs={{0,8},{4,12},{8,16},{12,20},{16,24},{20,28},{24,32},{28,36},{32,40... | collective-permute-start | bytes 1572872 | tf_op jit(solution)/shard_map/ppermute | solution.py:366
  90.3 43.2 %all-to-all-start.1 = ((bf16[32,64,128]{2,1,0:T(8,128)(2,1)}), bf16[32,64,128]{2,1,0:T(8,128)(2,1)S(1)}, u32[]{:S(2)}, u32[]{:S(2)}) async-start(bf16[32,64,128]{2,1,0:T(8,128)(2,1)} %delta_chain.1), calls=%async_computation.1 | async-start | bytes 1048576 | tf_op jit(solution)/shard_map/all_to_all | solution.py:455
  101.2 8.5 %copy-start.8 = (bf16[1,512,256]{2,1,0:T(8,128)(2,1)S(1)}, bf16[1,512,256]{2,1,0:T(8,128)(2,1)}, u32[]{:S(2)}) copy-start(bf16[1,512,256]{2,1,0:T(8,128)(2,1)} %copy-done.7) | copy-start | bytes 786436
  109.7 23.8 %copy-start.9 = (bf16[2,512,256]{2,1,0:T(8,128)(2,1)}, bf16[2,512,256]{2,1,0:T(8,128)(2,1)S(1)}, u32[]{:S(2)}) copy-start(bf16[2,512,256]{2,1,0:T(8,128)(2,1)S(1)} %collective-permute-done.kv2_ref) | copy-start | bytes 1572868
  109.8 31.9 %collective-permute-start.4 = (bf16[2,512,256]{2,1,0:T(8,128)(2,1)S(1)}, bf16[2,512,256]{2,1,0:T(8,128)(2,1)S(1)}, u32[]{:S(2)}, u32[]{:S(2)}) collective-permute-start(bf16[2,512,256]{2,1,0:T(8,128)(2,1)S(1)} %broadcast_select_fusion.2), channel_id=1, source_target_pairs={{0,4},{4,0},{8,12},{12,8},{16,20},{20,16},{24,28},{28,24},{32,36},... | collective-permute-start | bytes 1572872 | tf_op jit(solution)/shard_map/ppermute | solution.py:366
  133.5 0.8 copy-start.10
  141.7 0.8 copy-start.11
